TPU v7x, 128 devices: a whole 4x4x4 slice. The times are simulated.
128 devices in a mesh: rep: 2 (over core), exp: 32 (over z, x_lo, y), mdl: 2 (over x_hi).
Axes of the slice: x: 4 (x_hi: 2, x_lo: 2; x = x_hi * 2 + x_lo), y: 4, z: 4, core: 2. Of those that a mesh axis runs over, the one named last changes fastest.
Arguments:
- tokens_in: bfloat16 [12608, 768], P(('rep', 'exp')), may hold values from -6 to 6
- expert_ids: int32 [2, 12608, 2], P(None, ('rep', 'exp')), may hold values from 0 to 31, all different within a row; in each aligned block of 197 rows (0 to 196, 197 to 393, ..., all dimensions but the last counted through in order) at most 16 rows name the same one
- w_qkv: bfloat16 [2, 768, 3, 768], P(None, ('rep', 'exp'), None, 'mdl'), may hold values from -0.21875 to 0.21875
- w_out: bfloat16 [2, 768, 768], P(None, 'mdl', ('rep', 'exp')), may hold values from -1.75 to 1.75
- router: bfloat16 [2, 768, 32], P(None, ('rep', 'exp')), may hold values from -0.15625 to 0.15625
- gains: bfloat16 [2, 2, 768], P(None, None, ('rep', 'exp')), may hold values from 0.5 to 1.5
- shifts: bfloat16 [2, 3, 768], P(None, None, ('rep', 'exp')), may hold values from -1.1953125 to 1.1953125
- w_in: bfloat16 [2, 32, 768, 3072], P(None, 'exp', 'rep', 'mdl'), may hold values from -0.21875 to 0.21875
- b_in: bfloat16 [2, 32, 3072], P(None, 'exp', 'mdl'), may hold values from -1.796875 to 1.796875
- w_exp_out: bfloat16 [2, 32, 3072, 768], P(None, 'exp', 'mdl', 'rep'), may hold values from -0.109375 to 0.109375
- b_out: bfloat16 [2, 32, 768], P(None, 'exp', 'rep'), may hold values from -1.796875 to 1.796875
- cotangent: bfloat16 [12608, 768], P(('rep', 'exp')), may hold values from -6 to 6
Outputs:
- mixed: bfloat16 [12608, 768], P(('rep', 'exp'))
- grad_tokens: float32 [12608, 768], P(('rep', 'exp'))
- grad_w_qkv: float32 [2, 768, 3, 768], P(None, ('rep', 'exp'), None, 'mdl')
- grad_w_out: float32 [2, 768, 768], P(None, 'mdl', ('rep', 'exp'))
- grad_router: float32 [2, 768, 32], P(None, ('rep', 'exp'))
- grad_gains: float32 [2, 2, 768], P(None, None, ('rep', 'exp'))
- grad_shifts: float32 [2, 3, 768], P(None, None, ('rep', 'exp'))
- grad_w_in: float32 [2, 32, 768, 3072], P(None, 'exp', 'rep', 'mdl')
- grad_b_in: float32 [2, 32, 3072], P(None, 'exp', 'mdl')
- grad_w_exp_out: float32 [2, 32, 3072, 768], P(None, 'exp', 'mdl', 'rep')
- grad_b_out: float32 [2, 32, 768], P(None, 'exp', 'rep')
Inputs may be any that keep to these rules, and one draw needn't show every extreme that they name: `expert_ids`: in each block, among the 197 tokens of one aligned block of tokens, no expert is chosen more than 16 times, a bound that some block reaches; a token's two experts differ.
All inputs are finite; a program needn't handle non-finite values.
Results may differ from a plain program's by a relative error of at most 0.025.
Values may be sent and summed in bfloat16 or wider, within the bound.
A program may use at most 192 MiB of HBM per device.

v0:
```python
import jax
import jax.numpy as jnp
from jax import lax
from jax.experimental import pallas as pl
from jax.experimental.pallas import tpu as pltpu
from jax.sharding import PartitionSpec as P

HD = 64
SEQ = 197
EPSILON = 1e-06
F32 = jnp.float32
BF16 = jnp.bfloat16


def norm_rows(values, gain, shift):
    row_mean = jnp.mean(values, axis=-1, keepdims=True)
    centred = values - row_mean
    row_var = jnp.mean(centred * centred, axis=-1, keepdims=True)
    return centred * lax.rsqrt(row_var + EPSILON) * gain + shift


def dot(a, b):
    return jnp.dot(a, b, preferred_element_type=F32)


def dot_tn(a, b):
    return lax.dot_general(a, b, (((0,), (0,)), ((), ())), preferred_element_type=F32)


def dot_nt(a, b):
    return lax.dot_general(a, b, (((1,), (1,)), ((), ())), preferred_element_type=F32)


def other_core(values):
    return lax.ppermute(values, "rep", [(0, 1), (1, 0)])


def in_order(own, other, axis):
    first = lax.axis_index("rep") == 0
    return jnp.concatenate(
        [jnp.where(first, own, other), jnp.where(first, other, own)], axis=axis
    )


MESH = pl.DeviceIdType.MESH
BLOCK = 16
NEAR = 8
FAR = 4


def chip_place():
    rep = lax.axis_index("rep")
    exp = lax.axis_index("exp")
    near = (1 - rep) * (exp // 8 * 2 + exp // 4 % 2) + rep * (exp % 8)
    far = (1 - rep) * (exp % 4) + rep * (exp // 8)

    def chip_of(near_idx, far_idx):
        return (1 - rep) * (near_idx // 2 * 8 + near_idx % 2 * 4 + far_idx) + rep * (
            far_idx * 8 + near_idx
        )

    return rep, exp, near, far, chip_of


def greet(near, far, chip_of, rep):
    barrier = pltpu.get_barrier_semaphore()
    for step in range(1, NEAR):
        peer = chip_of((near + step) % NEAR, far)
        pl.semaphore_signal(barrier, inc=1, device_id={"exp": peer}, device_id_type=MESH)
    for step in range(1, FAR):
        peer = chip_of(near, (far + step) % FAR)
        pl.semaphore_signal(barrier, inc=1, device_id={"exp": peer}, device_id_type=MESH)
    pl.semaphore_signal(barrier, inc=1, device_id={"rep": 1 - rep}, device_id_type=MESH)
    pl.semaphore_wait(barrier, NEAR + FAR - 1)


def gather_kernel(
    mine,
    whole0,
    whole1,
    own_sem,
    near_send,
    near_recv,
    far_send,
    far_recv,
    core_send,
    core_recv,
):
    rep, exp, near, far, chip_of = chip_place()
    wholes = (whole0, whole1)

    def near_copy(layer, step, slot):
        return pltpu.make_async_remote_copy(
            src_ref=mine.at[layer],
            dst_ref=wholes[layer].at[rep, exp],
            send_sem=near_send.at[layer, step],
            recv_sem=near_recv.at[layer, slot],
            device_id={"exp": chip_of((near + step) % NEAR, far)},
            device_id_type=MESH,
        )

    def far_copy(layer, step, source, slot_near, slot_far):
        return pltpu.make_async_remote_copy(
            src_ref=wholes[layer].at[rep, source],
            dst_ref=wholes[layer].at[rep, source],
            send_sem=far_send.at[layer, step, slot_near],
            recv_sem=far_recv.at[layer, slot_far, slot_near],
            device_id={"exp": chip_of(near, (far + step) % FAR)},
            device_id_type=MESH,
        )

    def core_copy(layer, source, part):
        return pltpu.make_async_remote_copy(
            src_ref=wholes[layer].at[part, source],
            dst_ref=wholes[layer].at[part, source],
            send_sem=core_send.at[layer, source],
            recv_sem=core_recv.at[layer, source],
            device_id={"rep": 1 - rep},
            device_id_type=MESH,
        )

    keeps = [
        pltpu.make_async_copy(mine.at[layer], wholes[layer].at[rep, exp], own_sem.at[layer])
        for layer in range(2)
    ]
    for keep in keeps:
        keep.start()
    greet(near, far, chip_of, rep)
    for layer in range(2):

        @pl.loop(1, NEAR)
        def _(step):
            near_copy(layer, step, near).start()

    for keep in keeps:
        keep.wait()
    for layer in range(2):

        @pl.loop(0, NEAR)
        def _(back):
            slot = (near - back + NEAR) % NEAR
            source = chip_of(slot, far)

            @pl.when(back > 0)
            def _():
                near_copy(layer, back, slot).wait_recv()

            @pl.loop(1, FAR)
            def _(step):
                far_copy(layer, step, source, slot, far).start()

            core_copy(layer, source, rep).start()

    for layer in range(2):

        @pl.loop(0, NEAR)
        def _(back):
            slot = (near - back + NEAR) % NEAR

            @pl.loop(1, FAR)
            def _(step):
                slot_far = (far - step + FAR) % FAR
                source = chip_of(slot, slot_far)
                far_copy(layer, step, source, slot, slot_far).wait_recv()
                core_copy(layer, source, rep).start()

    for layer in range(2):

        @pl.loop(0, NEAR * FAR)
        def _(source):
            core_copy(layer, source, 1 - rep).wait_recv()
            core_copy(layer, source, rep).wait_send()

        @pl.loop(1, NEAR)
        def _(step):
            near_copy(layer, step, near).wait_send()

        @pl.loop(1, FAR)
        def _(step):
            @pl.loop(0, NEAR)
            def _(slot):
                far_copy(layer, step, chip_of(slot, far), slot, far).wait_send()


def gather_weights(packed):
    layers, rows, cols = packed.shape
    whole = jax.ShapeDtypeStruct((2, NEAR * FAR, rows, cols), BF16)
    got = pl.pallas_call(
        gather_kernel,
        out_shape=(whole, whole),
        in_specs=[pl.BlockSpec(memory_space=pl.ANY)],
        out_specs=(pl.BlockSpec(memory_space=pl.ANY), pl.BlockSpec(memory_space=pl.ANY)),
        scratch_shapes=[
            pltpu.SemaphoreType.DMA((2,)),
            pltpu.SemaphoreType.DMA((2, NEAR)),
            pltpu.SemaphoreType.DMA((2, NEAR)),
            pltpu.SemaphoreType.DMA((2, FAR, NEAR)),
            pltpu.SemaphoreType.DMA((2, FAR, NEAR)),
            pltpu.SemaphoreType.DMA((2, NEAR * FAR)),
            pltpu.SemaphoreType.DMA((2, NEAR * FAR)),
        ],
        compiler_params=pltpu.CompilerParams(collective_id=0, has_side_effects=True),
        name="gather_weights",
    )(packed)
    return [value.reshape(2 * NEAR * FAR * rows, cols) for value in got]


def scatter_kernel(
    h_one,
    grad_attended,
    h_two,
    rhs_qkv,
    rhs_proj,
    rhs_small,
    sums_in,
    spread,
    out,
    lhs_qkv,
    lhs_proj,
    lhs_small,
    sums,
    part,
    from_core,
    from_far,
    total,
    from_near,
    core_send,
    core_recv,
    far_send,
    far_recv,
    near_send,
    near_recv,
):
    rep, exp, near, far, chip_of = chip_place()
    qkv_cols, proj_cols = rhs_qkv.shape[1], rhs_proj.shape[1]
    cut = qkv_cols + proj_cols
    rows = BLOCK * 4
    chunks = NEAR * FAR // 4

    def multiply(core, chunk):
        at = pl.ds(pl.multiple_of((core * chunks + chunk) * rows, rows), rows)
        to = pl.ds(pl.multiple_of(chunk * rows, rows), rows)
        low = lambda lhs, rhs: jnp.dot(
            lhs[at, :], rhs[...], preferred_element_type=F32
        )
        part[core, to, :qkv_cols] = low(lhs_qkv, rhs_qkv).astype(BF16)
        part[core, to, qkv_cols:cut] = low(lhs_proj, rhs_proj).astype(BF16)
        part[core, to, cut:] = (low(lhs_small, rhs_small) + sums[at, :]).astype(BF16)

    def core_copy(chunk):
        to = pl.ds(pl.multiple_of(chunk * rows, rows), rows)
        return pltpu.make_async_remote_copy(
            src_ref=part.at[1 - rep, to],
            dst_ref=from_core.at[to],
            send_sem=core_send.at[chunk],
            recv_sem=core_recv.at[chunk],
            device_id={"rep": 1 - rep},
            device_id_type=MESH,
        )

    def far_copy(step, slot):
        return pltpu.make_async_remote_copy(
            src_ref=part.at[rep, block(chip_of(slot, (far + step) % FAR))],
            dst_ref=from_far.at[step, block(slot)],
            send_sem=far_send.at[step, slot],
            recv_sem=far_recv.at[step, slot],
            device_id={"exp": chip_of(near, (far + step) % FAR)},
            device_id_type=MESH,
        )

    def near_copy(step):
        return pltpu.make_async_remote_copy(
            src_ref=total.at[block((near + step) % NEAR)],
            dst_ref=from_near.at[step],
            send_sem=near_send.at[step],
            recv_sem=near_recv.at[step],
            device_id={"exp": chip_of((near + step) % NEAR, far)},
            device_id_type=MESH,
        )

    lhs_qkv[...] = dot_nt(spread[...], h_one[...]).astype(BF16)
    lhs_proj[...] = dot_nt(spread[...], grad_attended[...]).astype(BF16)
    lhs_small[...] = dot_nt(spread[...], h_two[...]).astype(BF16)
    sums[...] = dot_nt(spread[...], sums_in[...].astype(BF16))
    greet(near, far, chip_of, rep)

    @pl.loop(0, chunks)
    def _(chunk):
        multiply(1 - rep, chunk)
        core_copy(chunk).start()

    @pl.loop(0, chunks)
    def _(chunk):
        multiply(rep, chunk)

    @pl.loop(0, chunks)
    def _(chunk):
        to = pl.ds(pl.multiple_of(chunk * rows, rows), rows)
        core_copy(chunk).wait_recv()
        part[rep, to, :] = (
            part[rep, to, :].astype(F32) + from_core[to, :].astype(F32)
        ).astype(BF16)

    @pl.loop(1, FAR)
    def _(step):
        @pl.loop(1, NEAR + 1)
        def _(ahead):
            far_copy(step, (near + ahead) % NEAR).start()

    def add_far(slot):
        for step in range(1, FAR):
            far_copy(step, slot).wait_recv()
        value = part[rep, block(chip_of(slot, far)), :].astype(F32)
        for step in range(1, FAR):
            value = value + from_far[step, block(slot), :].astype(F32)
        return value

    @pl.loop(1, NEAR)
    def _(step):
        slot = (near + step) % NEAR
        total[block(slot), :] = add_far(slot).astype(BF16)
        near_copy(step).start()

    out[...] = add_far(near)

    @pl.loop(1, NEAR)
    def _(step):
        near_copy(step).wait_recv()
        out[...] += from_near[step].astype(F32)

    @pl.loop(1, NEAR)
    def _(step):
        near_copy(step).wait_send()

    @pl.loop(1, FAR)
    def _(step):
        @pl.loop(0, NEAR)
        def _(slot):
            far_copy(step, slot).wait_send()

    @pl.loop(0, chunks)
    def _(chunk):
        core_copy(chunk).wait_send()


def scatter_grads(lhs, rhs, sums, spread):
    cols = sum(r.shape[1] for r in rhs)
    half = NEAR * FAR * BLOCK
    tokens = lhs[0].shape[0]
    return pl.pallas_call(
        scatter_kernel,
        out_shape=jax.ShapeDtypeStruct((BLOCK, cols), F32),
        in_specs=[pl.BlockSpec(memory_space=pltpu.VMEM)] * 8,
        out_specs=pl.BlockSpec(memory_space=pltpu.VMEM),
        scratch_shapes=[
            pltpu.VMEM((2 * half, tokens), BF16),
            pltpu.VMEM((2 * half, tokens), BF16),
            pltpu.VMEM((2 * half, tokens), BF16),
            pltpu.VMEM((2 * half, 128), F32),
            pltpu.VMEM((2, half, cols), BF16),
            pltpu.VMEM((half, cols), BF16),
            pltpu.VMEM((FAR, NEAR * BLOCK, cols), BF16),
            pltpu.VMEM((NEAR * BLOCK, cols), BF16),
            pltpu.VMEM((NEAR, BLOCK, cols), BF16),
            pltpu.SemaphoreType.DMA((half // BLOCK // 4,)),
            pltpu.SemaphoreType.DMA((half // BLOCK // 4,)),
            pltpu.SemaphoreType.DMA((FAR, NEAR)),
            pltpu.SemaphoreType.DMA((FAR, NEAR)),
            pltpu.SemaphoreType.DMA((NEAR,)),
            pltpu.SemaphoreType.DMA((NEAR,)),
        ],
        compiler_params=pltpu.CompilerParams(
            collective_id=1, has_side_effects=True, vmem_limit_bytes=40 << 20
        ),
        name="scatter_grads",
    )(*lhs, *rhs, sums, spread)


PLANES = 4
PLANE = 8


def block(source):
    return pl.ds(pl.multiple_of(source * BLOCK, BLOCK), BLOCK)


def plane_rows(plane):
    return pl.ds(pl.multiple_of(plane * (PLANE * BLOCK), PLANE * BLOCK), PLANE * BLOCK)


def plane_step(turn):
    return turn + turn // 2 - 2 * (turn // 3)


def greet_all(exp):
    barrier = pltpu.get_barrier_semaphore()

    @pl.loop(1, PLANES * PLANE)
    def _(step):
        peer = (exp + step) % (PLANES * PLANE)
        pl.semaphore_signal(barrier, inc=1, device_id={"exp": peer}, device_id_type=MESH)

    mdl = lax.axis_index("mdl")
    pl.semaphore_signal(barrier, inc=1, device_id={"mdl": 1 - mdl}, device_id_type=MESH)
    return barrier


def core_send_copy(src, dst, sems, idx):
    return pltpu.make_async_remote_copy(
        src_ref=src,
        dst_ref=dst,
        send_sem=sems.at[idx, 0],
        recv_sem=sems.at[idx, 1],
        device_id={"rep": 1 - lax.axis_index("rep")},
        device_id_type=MESH,
    )


def half_copy(src, dst, sems, idx):
    return pltpu.make_async_remote_copy(
        src_ref=src,
        dst_ref=dst,
        send_sem=sems.at[idx, 0],
        recv_sem=sems.at[idx, 1],
        device_id={"mdl": 1 - lax.axis_index("mdl")},
        device_id_type=MESH,
    )


def row_copy(src, dst, exp, send_sem, recv_sem, peer, source):
    return pltpu.make_async_remote_copy(
        src_ref=src.at[block(peer)],
        dst_ref=dst.at[block(exp)],
        send_sem=send_sem.at[peer],
        recv_sem=recv_sem.at[source],
        device_id={"exp": peer},
        device_id_type=MESH,
    )


def send_all(src, dst, exp, send_sem, recv_sem):
    @pl.loop(0, PLANES)
    def _(turn):
        plane = (exp // PLANE + plane_step(turn)) % PLANES

        @pl.loop(0, PLANE)
        def _(step):
            peer = plane * PLANE + (exp + step) % PLANE

            @pl.when(turn + step > 0)
            def _():
                row_copy(src, dst, exp, send_sem, recv_sem, peer, exp).start()

    dst[block(exp), :] = src[block(exp), :]


def each_plane(src, back_src, dst, back_dst, exp, sems, work):
    send_sem, recv_sem, back_send, back_recv = sems

    @pl.loop(0, PLANES)
    def _(turn):
        plane = (exp // PLANE - plane_step(turn) + PLANES) % PLANES

        @pl.loop(0, PLANE)
        def _(step):
            source = plane * PLANE + (exp - step + PLANE) % PLANE

            @pl.when(turn + step > 0)
            def _():
                row_copy(src, dst, exp, send_sem, recv_sem, source, source).wait_recv()

        work(plane_rows(plane))

        @pl.loop(0, PLANE)
        def _(step):
            source = plane * PLANE + (exp - step + PLANE) % PLANE

            @pl.when(turn + step > 0)
            def _():
                row_copy(back_src, back_dst, exp, back_send, back_recv, source, exp).start()

    back_dst[block(exp), :] = back_src[block(exp), :]


def wait_back(back_src, back_dst, exp, sems):
    @pl.loop(1, PLANES * PLANE)
    def _(step):
        source = (exp + step) % (PLANES * PLANE)
        row_copy(back_src, back_dst, exp, sems[2], sems[3], source, source).wait_recv()


def wait_sent(src, dst, back_src, back_dst, exp, sems):
    @pl.loop(1, PLANES * PLANE)
    def _(step):
        peer = (exp + step) % (PLANES * PLANE)
        row_copy(src, dst, exp, sems[0], sems[1], peer, peer).wait_send()
        row_copy(back_src, back_dst, exp, sems[2], sems[3], peer, peer).wait_send()


def weight_loads(own_in, other_in, own_out, other_out, w_in, w_out):
    rep = lax.axis_index("rep")
    depth = own_in.shape[0]
    pairs = []
    for src_in, src_out, core in ((own_in, own_out, rep), (other_in, other_out, 1 - rep)):
        place = pl.ds(pl.multiple_of(core * depth, 128), depth)
        pairs.append((src_in, w_in.at[place, :]))
        pairs.append((src_out, w_out.at[:, place]))
    return pairs


def lanes(values):
    rows = values[0].shape[0]
    lane = lax.broadcasted_iota(jnp.int32, (rows, 128), 1)
    total = jnp.zeros((rows, 128), F32)
    for idx, value in enumerate(values):
        total = jnp.where(lane == idx, value, total)
    return total


VMEM_SPEC = pl.BlockSpec(memory_space=pltpu.VMEM)
ANY_SPEC = pl.BlockSpec(memory_space=pl.ANY)
SMALL = 128


def row_sems():
    return [pltpu.SemaphoreType.DMA((PLANES * PLANE,))] * 4


def head_slices(head, width):
    start = head * HD
    return [slice(part * width + start, part * width + start + HD) for part in range(3)]


def masked_scores(query_rows, key_rows):
    scores = dot_nt(query_rows, key_rows) * HD ** (-0.5)
    col = lax.broadcasted_iota(jnp.int32, scores.shape, 1)
    return jnp.where(col < SEQ, scores, -1e30)


def attend_forward(qkv, heads, log_total):
    width = heads.shape[1]
    totals = []
    for head in range(width // HD):
        q_at, k_at, v_at = head_slices(head, width)
        scores = masked_scores(qkv[:, q_at], qkv[:, k_at])
        top_score = jnp.max(scores, axis=-1, keepdims=True)
        raw_weight = jnp.exp(scores - top_score)
        row_total = jnp.sum(raw_weight, axis=-1, keepdims=True)
        probs_low = (raw_weight / row_total).astype(BF16)
        totals.append(top_score + jnp.log(row_total))
        heads[:, q_at] = dot(probs_low, qkv[:, v_at]).astype(BF16)
    log_total[...] = lanes(totals)


def attend_backward(grad_heads, qkv, log_total, grad_qkv):
    width = grad_heads.shape[1]
    for head in range(width // HD):
        q_at, k_at, v_at = head_slices(head, width)
        query_rows, key_rows, value_rows = qkv[:, q_at], qkv[:, k_at], qkv[:, v_at]
        grad_out = grad_heads[:, q_at]
        probs = jnp.exp(masked_scores(query_rows, key_rows) - log_total[:, head : head + 1])
        grad_probs = dot_nt(grad_out, value_rows)
        grad_scores = probs * (grad_probs - jnp.sum(grad_probs * probs, axis=-1, keepdims=True))
        grad_scores = grad_scores.astype(BF16)
        grad_qkv[:, q_at] = (dot(grad_scores, key_rows) * HD ** (-0.5)).astype(BF16)
        grad_qkv[:, k_at] = (dot_tn(grad_scores, query_rows) * HD ** (-0.5)).astype(BF16)
        grad_qkv[:, v_at] = dot_tn(probs.astype(BF16), grad_out).astype(BF16)


def block_forward_kernel(
    state,
    spread,
    turned,
    pick0,
    pick1,
    hot0,
    hot1,
    b_in,
    b_out,
    whole_in,
    own_in,
    other_in,
    own_out,
    other_out,
    after_out,
    h_out,
    gates_out,
    picked0_out,
    picked1_out,
    next_out,
    h_one_out,
    qkv_out,
    log_out,
    heads_out,
    rows_out,
    slope_out,
    active_out,
    whole,
    w_in,
    w_out,
    send,
    rows,
    slope,
    active,
    back_src,
    back,
    own_att,
    low_att,
    own_moe,
    low_moe,
    load_sems,
    out_sems,
    half_sems,
    send_sem,
    recv_sem,
    back_send,
    back_recv,
):
    exp = lax.axis_index("exp")
    sems = (send_sem, recv_sem, back_send, back_recv)
    loads = [
        pltpu.make_async_copy(src, dst, load_sems.at[idx])
        for idx, (src, dst) in enumerate(
            [(whole_in, whole)]
            + weight_loads(own_in, other_in, own_out, other_out, w_in, w_out)
        )
    ]
    for load in loads:
        load.start()
    barrier = greet_all(exp)
    qkv_cols = qkv_out.shape[1]
    cut = qkv_cols + heads_out.shape[1]
    loads[0].wait()
    small = dot_tn(whole[:, cut:], spread[...])
    first_row = PLANES * PLANE
    gain0, gain1, shift0, shift1, shift2 = [
        small[first_row + idx : first_row + idx + 1, :] for idx in range(5)
    ]
    h_one = norm_rows(state[...], gain0, shift0).astype(BF16)
    h_one_out[...] = h_one
    wide = dot_nt(h_one, spread[...]).astype(BF16)
    qkv_out[...] = dot(wide, whole[:, :qkv_cols]).astype(BF16)
    attend_forward(qkv_out, heads_out, log_out)
    own_att[...] = dot(
        dot_nt(heads_out[...], whole[:, qkv_cols:cut]).astype(BF16), spread[...]
    ).astype(BF16)
    pl.semaphore_wait(barrier, PLANES * PLANE)
    first = half_copy(own_att, low_att, half_sems, 0)
    first.start()
    first.wait_recv()
    after = state[...] + (own_att[...].astype(F32) + low_att[...].astype(F32)) + shift2
    after_out[...] = after
    h_two = norm_rows(after, gain1, shift1).astype(BF16)
    h_out[...] = h_two
    send[...] = dot(turned[...], h_two).astype(BF16)
    send_all(send, rows, exp, send_sem, recv_sem)
    logits = dot_nt(h_two, small.astype(BF16))
    chosen = [jnp.sum(logits * hot[...].astype(F32), axis=1, keepdims=True) for hot in (hot0, hot1)]
    top = jnp.maximum(chosen[0], chosen[1])
    raw = [jnp.exp(value - top) for value in chosen]
    gates = [value / (raw[0] + raw[1]) for value in raw]
    gates_out[...] = lanes(gates)
    bias_in = b_in[...].astype(F32)
    for load in loads[1:]:
        load.wait()
    tile = 512

    def work(at):
        for col in range(0, active.shape[1], tile):
            cols = slice(col, col + tile)
            inner = dot(rows[at, :], w_in[:, cols]) + bias_in[:, cols]
            cdf = 0.5 * (1.0 + lax.erf(inner * (0.5**0.5)))
            active[at, cols] = (inner * cdf).astype(BF16)
            slope[at, cols] = (
                cdf + inner * jnp.exp(-0.5 * inner * inner) * 0.3989422804014327
            ).astype(BF16)
        back_src[at, :] = (dot(active[at, :], w_out[...]) + b_out[...]).astype(BF16)

    each_plane(send, back_src, rows, back, exp, sems, work)
    saves = [
        pltpu.make_async_copy(src, dst, out_sems.at[idx])
        for idx, (src, dst) in enumerate(
            ((rows, rows_out), (slope, slope_out), (active, active_out))
        )
    ]
    for save in saves:
        save.start()
    wait_back(back_src, back, exp, sems)
    picked = [dot(pick[...], back[...]) for pick in (pick0, pick1)]
    own_moe[...] = (gates[0] * picked[0] + gates[1] * picked[1]).astype(BF16)
    second = half_copy(own_moe, low_moe, half_sems, 1)
    second.start()
    picked0_out[...] = picked[0].astype(BF16)
    picked1_out[...] = picked[1].astype(BF16)
    wait_sent(send, rows, back_src, back, exp, sems)
    second.wait_recv()
    next_out[...] = after_out[...] + (own_moe[...].astype(F32) + low_moe[...].astype(F32))
    first.wait_send()
    second.wait_send()
    for save in saves:
        save.wait()


def block_forward(near, whole, weights):
    tokens, width = near[0].shape
    slots = near[2].shape[0]
    hidden = weights[0].shape[1]
    cols = whole.shape[1]
    proj = (cols - SMALL) // 4
    shape = jax.ShapeDtypeStruct
    return pl.pallas_call(
        block_forward_kernel,
        out_shape=(
            shape((tokens, width), F32),
            shape((tokens, width), BF16),
            shape((tokens, 128), F32),
            shape((tokens, width), BF16),
            shape((tokens, width), BF16),
            shape((tokens, width), F32),
            shape((tokens, width), BF16),
            shape((tokens, 3 * proj), BF16),
            shape((tokens, 128), F32),
            shape((tokens, proj), BF16),
            shape((slots, width), BF16),
            shape((slots, hidden), BF16),
            shape((slots, hidden), BF16),
        ),
        in_specs=[VMEM_SPEC] * 9 + [ANY_SPEC] * 5,
        out_specs=tuple([VMEM_SPEC] * 10 + [ANY_SPEC] * 3),
        scratch_shapes=[
            pltpu.VMEM(whole.shape, BF16),
            pltpu.VMEM((width, hidden), BF16),
            pltpu.VMEM((hidden, width), BF16),
            pltpu.VMEM((slots, width), BF16),
            pltpu.VMEM((slots, width), BF16),
            pltpu.VMEM((slots, hidden), BF16),
            pltpu.VMEM((slots, hidden), BF16),
            pltpu.VMEM((slots, width), BF16),
            pltpu.VMEM((slots, width), BF16),
        ]
        + [pltpu.VMEM((tokens, width), BF16)] * 4
        + [
            pltpu.SemaphoreType.DMA((5,)),
            pltpu.SemaphoreType.DMA((3,)),
            pltpu.SemaphoreType.DMA((2, 2)),
        ]
        + row_sems(),
        compiler_params=pltpu.CompilerParams(
            collective_id=2, has_side_effects=True, vmem_limit_bytes=56 << 20
        ),
        name="block_forward",
    )(*near, whole, *weights)


def norm_parts(values):
    row_mean = jnp.mean(values, axis=-1, keepdims=True)
    centred = values - row_mean
    row_var = jnp.mean(centred * centred, axis=-1, keepdims=True)
    scale = lax.rsqrt(row_var + EPSILON)
    return centred * scale, scale


def norm_grad(grad, unit, scale, gain):
    scaled = grad * gain
    return scale * (
        scaled
        - jnp.mean(scaled, axis=-1, keepdims=True)
        - unit * jnp.mean(scaled * unit, axis=-1, keepdims=True)
    )


def block_backward_kernel(
    grad_state,
    spread,
    gates,
    picked0,
    picked1,
    turned0,
    turned1,
    pick,
    hot0,
    hot1,
    after,
    state_in,
    qkv,
    log_total,
    heads,
    whole_in,
    own_in,
    other_in,
    own_out,
    other_out,
    slope_in,
    active_in,
    rows_in,
    grad_out,
    grad_att_out,
    grad_logits_out,
    sums_out,
    grad_qkv_out,
    grad_in_out,
    grad_exp_out,
    grad_b_in_out,
    grad_b_out_out,
    whole,
    w_in,
    w_out,
    slope,
    active,
    kept_rows,
    send,
    rows,
    inner,
    back_src,
    back,
    own_gate,
    low_gate,
    own_h,
    low_h,
    own_one,
    low_one,
    product,
    in_away,
    in_got,
    exp_away,
    exp_got,
    bias_own,
    bias_got,
    grad_heads,
    load_sems,
    half_sems,
    core_sems,
    send_sem,
    recv_sem,
    back_send,
    back_recv,
):
    exp = lax.axis_index("exp")
    rep = lax.axis_index("rep")
    sems = (send_sem, recv_sem, back_send, back_recv)
    loads = [
        pltpu.make_async_copy(src, dst, load_sems.at[idx])
        for idx, (src, dst) in enumerate(
            weight_loads(own_in, other_in, own_out, other_out, w_in, w_out)
            + [
                (slope_in, slope),
                (whole_in, whole),
                (active_in, active),
                (rows_in, kept_rows),
            ]
        )
    ]
    for load in loads:
        load.start()
    barrier = greet_all(exp)
    pl.semaphore_signal(barrier, inc=1, device_id={"rep": 1 - rep}, device_id_type=MESH)
    grad = grad_state[...]
    gate0, gate1 = gates[:, 0:1], gates[:, 1:2]
    send[...] = (
        dot(turned0[...], (gate0 * grad).astype(BF16))
        + dot(turned1[...], (gate1 * grad).astype(BF16))
    ).astype(BF16)
    pl.semaphore_wait(barrier, PLANES * PLANE + 1)
    send_all(send, rows, exp, send_sem, recv_sem)
    own_gate[...] = lanes(
        [
            jnp.sum(grad * picked[...].astype(F32), axis=1, keepdims=True)
            for picked in (picked0, picked1)
        ]
    )
    first = half_copy(own_gate, low_gate, half_sems, 0)
    first.start()
    for load in loads:
        load.wait()
    qkv_cols = qkv.shape[1]
    cut = qkv_cols + heads.shape[1]
    small = dot_tn(whole[:, cut:], spread[...])
    first_row = PLANES * PLANE
    gain0, gain1 = [small[first_row + idx : first_row + idx + 1, :] for idx in range(2)]

    def work(at):
        grad_active = dot_nt(rows[at, :], w_out[...])
        inner[at, :] = (grad_active * slope[at, :].astype(F32)).astype(BF16)
        back_src[at, :] = dot_nt(inner[at, :], w_in[...]).astype(BF16)

    each_plane(send, back_src, rows, back, exp, sems, work)

    half = grad_in_out.shape[0]
    hidden = inner.shape[1]
    own_at = pl.ds(pl.multiple_of(rep * half, 128), half)
    other_at = pl.ds(pl.multiple_of((1 - rep) * half, 128), half)
    in_away[...] = dot_tn(kept_rows[:, other_at], inner[...]).astype(BF16)
    in_copy = core_send_copy(in_away, in_got, core_sems, 0)
    in_copy.start()
    tall = product.shape[0]
    for start in range(0, hidden, tall):
        part = slice(start, start + tall)
        product[...] = dot_tn(active[:, part], rows[...])
        grad_exp_out[part, :] = product[:, own_at]
        exp_away[part, :] = product[:, other_at].astype(BF16)
    exp_copy = core_send_copy(exp_away, exp_got, core_sems, 1)
    exp_copy.start()
    bias_own[...] = jnp.zeros_like(bias_own)
    bias_own[0:1, :hidden] = jnp.sum(inner[...].astype(F32), axis=0, keepdims=True)
    bias_own[0:1, hidden:] = jnp.sum(rows[...].astype(F32), axis=0, keepdims=True)
    bias_copy = core_send_copy(bias_own, bias_got, core_sems, 2)
    bias_copy.start()
    grad_in_out[...] = dot_tn(kept_rows[:, own_at], inner[...])

    first.wait_recv()
    total = own_gate[...] + low_gate[...]
    grad0, grad1 = total[:, 0:1], total[:, 1:2]
    mean = gate0 * grad0 + gate1 * grad1
    grad_logits = (
        gate0 * (grad0 - mean) * hot0[...].astype(F32)
        + gate1 * (grad1 - mean) * hot1[...].astype(F32)
    ).astype(BF16)
    grad_logits_out[...] = grad_logits
    from_router = dot(grad_logits, small.astype(BF16))
    unit, scale = norm_parts(after[...])
    wait_back(back_src, back, exp, sems)
    own_h[...] = dot(pick[...], back[...]).astype(BF16)
    second = half_copy(own_h, low_h, half_sems, 1)
    second.start()
    in_copy.wait_recv()
    grad_in_out[...] += in_got[...].astype(F32)
    exp_copy.wait_recv()
    grad_exp_out[...] += exp_got[...].astype(F32)
    bias_copy.wait()
    bias_own[...] += bias_got[...]
    grad_b_in_out[...] = bias_own[0:1, :hidden]
    grad_b_out_out[...] = bias_own[
        0:1, pl.ds(pl.multiple_of(hidden + rep * half, 128), half)
    ]
    wait_sent(send, rows, back_src, back, exp, sems)
    second.wait_recv()
    grad_h = own_h[...].astype(F32) + low_h[...].astype(F32) + from_router
    grad_after = norm_grad(grad_h, unit, scale, gain1) + grad_state[...]
    grad_att = grad_after.astype(BF16)
    grad_att_out[...] = grad_att
    sums_out[...] = jnp.zeros_like(sums_out)
    put = lambda idx, value: sums_out.__setitem__(
        (slice(first_row + idx, first_row + idx + 1), slice(None)),
        jnp.sum(value, axis=0, keepdims=True),
    )
    put(1, grad_h * unit)
    put(3, grad_h)
    put(4, grad_after)
    wide = dot_nt(grad_att, spread[...]).astype(BF16)
    grad_heads[...] = dot(wide, whole[:, qkv_cols:cut]).astype(BF16)
    attend_backward(grad_heads, qkv, log_total, grad_qkv_out)
    own_one[...] = dot(
        dot_nt(grad_qkv_out[...], whole[:, :qkv_cols]).astype(BF16), spread[...]
    ).astype(BF16)
    third = half_copy(own_one, low_one, half_sems, 2)
    third.start()
    unit, scale = norm_parts(state_in[...])
    third.wait_recv()
    grad_one = own_one[...].astype(F32) + low_one[...].astype(F32)
    grad_out[...] = grad_after + norm_grad(grad_one, unit, scale, gain0)
    put(0, grad_one * unit)
    put(2, grad_one)
    for copy in (first, second, third, in_copy, exp_copy):
        copy.wait_send()


def block_backward(near, whole, weights, kept):
    tokens, width = near[0].shape
    slots = near[5].shape[0]
    hidden = weights[0].shape[1]
    cols = whole.shape[1]
    proj = (cols - SMALL) // 4
    half = width // 2
    shape = jax.ShapeDtypeStruct
    return pl.pallas_call(
        block_backward_kernel,
        out_shape=(
            shape((tokens, width), F32),
            shape((tokens, width), BF16),
            shape((tokens, 128), BF16),
            shape((128, width), F32),
            shape((tokens, 3 * proj), BF16),
            shape((half, hidden), F32),
            shape((hidden, half), F32),
            shape((1, hidden), F32),
            shape((1, half), F32),
        ),
        in_specs=[VMEM_SPEC] * 15 + [ANY_SPEC] * 8,
        out_specs=tuple([VMEM_SPEC] * 9),
        scratch_shapes=[
            pltpu.VMEM(whole.shape, BF16),
            pltpu.VMEM((width, hidden), BF16),
            pltpu.VMEM((hidden, width), BF16),
            pltpu.VMEM((slots, hidden), BF16),
            pltpu.VMEM((slots, hidden), BF16),
            pltpu.VMEM((slots, width), BF16),
            pltpu.VMEM((slots, width), BF16),
            pltpu.VMEM((slots, width), BF16),
            pltpu.VMEM((slots, hidden), BF16),
            pltpu.VMEM((slots, width), BF16),
            pltpu.VMEM((slots, width), BF16),
            pltpu.VMEM((tokens, 128), F32),
            pltpu.VMEM((tokens, 128), F32),
        ]
        + [pltpu.VMEM((tokens, width), BF16)] * 4
        + [
            pltpu.VMEM((512, width), F32),
            pltpu.VMEM((half, hidden), BF16),
            pltpu.VMEM((half, hidden), BF16),
            pltpu.VMEM((hidden, half), BF16),
            pltpu.VMEM((hidden, half), BF16),
            pltpu.VMEM((8, hidden + width), F32),
            pltpu.VMEM((8, hidden + width), F32),
            pltpu.VMEM((tokens, proj), BF16),
            pltpu.SemaphoreType.DMA((8,)),
            pltpu.SemaphoreType.DMA((3, 2)),
            pltpu.SemaphoreType.DMA((3, 2)),
        ]
        + row_sems(),
        compiler_params=pltpu.CompilerParams(
            collective_id=3, has_side_effects=True, vmem_limit_bytes=56 << 20
        ),
        name="block_backward",
    )(*near, whole, *weights, *kept)


def on_device(
    tokens_in,
    expert_ids,
    w_qkv,
    w_out,
    router,
    gains,
    shifts,
    w_in,
    b_in,
    w_exp_out,
    b_out,
    cotangent,
):
    tok_rows, width = tokens_in.shape
    exp_count = lax.axis_size("exp")
    experts = w_in.shape[1] * exp_count
    capacity = 2 * tok_rows // experts + 4
    score_scale = HD ** (-0.5)
    layers = w_qkv.shape[0]
    own_rows = w_qkv.shape[1]
    qkv_cols = 3 * w_qkv.shape[3]
    out_cols = w_out.shape[1]
    small_cols = 128
    slot_count = experts * capacity

    packed = jnp.concatenate(
        [
            w_qkv.reshape(layers, own_rows, qkv_cols),
            jnp.swapaxes(w_out, 1, 2),
            router,
            jnp.swapaxes(gains, 1, 2),
            jnp.swapaxes(shifts, 1, 2),
            jnp.zeros((layers, own_rows, small_cols - experts - 5), BF16),
        ],
        axis=2,
    )
    packed = jnp.pad(packed, ((0, 0), (0, BLOCK - own_rows), (0, 0)))
    wholes = gather_weights(packed)
    expert_w = []
    for layer_idx in range(layers):
        own_in, own_out = w_in[layer_idx, 0], w_exp_out[layer_idx, 0]
        expert_w.append((own_in, other_core(own_in), own_out, other_core(own_out)))
    padded = wholes[0].shape[0]
    pad_row = jnp.arange(padded, dtype=jnp.int32)
    true_row = jnp.where(
        pad_row % BLOCK < own_rows, pad_row // BLOCK * own_rows + pad_row % BLOCK, -1
    )
    spread = (true_row[:, None] == jnp.arange(width, dtype=jnp.int32)).astype(BF16)
    out_bias = 0.5 * in_order(b_out, other_core(b_out), 2).astype(F32)

    tokens_pad = -(-tok_rows // BLOCK) * BLOCK
    spare = tokens_pad - tok_rows
    expert_cols = jnp.arange(128, dtype=jnp.int32)
    slot_cols = jnp.arange(slot_count, dtype=jnp.int32)
    row_idx = jnp.arange(tokens_pad, dtype=jnp.int32)
    before = (row_idx[:, None] > row_idx[None, :]).astype(BF16)

    def route(ids):
        ids = jnp.pad(ids, ((0, spare), (0, 0)), constant_values=-1)
        hot = [(ids[:, k : k + 1] == expert_cols).astype(BF16) for k in range(2)]
        earlier = dot(before, hot[0] + hot[1])
        picks = []
        turned = []
        for k in range(2):
            within = jnp.sum(earlier * hot[k].astype(F32), axis=1).astype(jnp.int32)
            slots = ids[:, k] * capacity + within
            picks.append((slots[:, None] == slot_cols).astype(BF16))
            turned.append((slots[None, :] == slot_cols[:, None]).astype(BF16))
        return hot, picks, turned, turned[0] + turned[1], picks[0] + picks[1]

    routed = [route(expert_ids[i]) for i in range(layers)]

    state = jnp.pad(tokens_in.astype(F32), ((0, spare), (0, 0)))
    saved = []
    for layer_idx in range(layers):
        hot, picks, turned, turned_both, picks_both = routed[layer_idx]
        got = block_forward(
            (
                state,
                spread,
                turned_both,
                picks[0],
                picks[1],
                hot[0],
                hot[1],
                b_in[layer_idx],
                out_bias[layer_idx],
            ),
            wholes[layer_idx],
            expert_w[layer_idx],
        )
        saved.append((state,) + tuple(got))
        state = got[5]
    mixed = state[:tok_rows].astype(BF16)
    grad_state = jnp.pad(cotangent.astype(F32), ((0, spare), (0, 0)))
    attn_grads = [None] * layers
    expert_grads = [None] * layers
    for layer_idx in reversed(range(layers)):
        hot, picks, turned, turned_both, picks_both = routed[layer_idx]
        (
            state_in,
            after,
            h_two,
            gates,
            picked0,
            picked1,
            _,
            h_one,
            qkv,
            log_total,
            heads,
            rows_in,
            slope,
            active,
        ) = saved[layer_idx]
        grad_state, grad_att, grad_logits, sums, grad_qkv, *expert_grads[layer_idx] = (
            block_backward(
                (
                    grad_state,
                    spread,
                    gates,
                    picked0,
                    picked1,
                    turned[0],
                    turned[1],
                    picks_both,
                    hot[0],
                    hot[1],
                    after,
                    state_in,
                    qkv,
                    log_total,
                    heads,
                ),
                wholes[layer_idx],
                expert_w[layer_idx],
                (slope, active, rows_in),
            )
        )
        attn_grads[layer_idx] = scatter_grads(
            (h_one, grad_att, h_two), (grad_qkv, heads, grad_logits), sums, spread
        )[:own_rows]
    grads = jnp.stack(attn_grads)
    small = grads[:, :, qkv_cols + out_cols :]
    return (
        mixed,
        grad_state[:tok_rows],
        grads[:, :, :qkv_cols].reshape(w_qkv.shape),
        jnp.swapaxes(grads[:, :, qkv_cols : qkv_cols + out_cols], 1, 2),
        small[:, :, :experts],
        jnp.swapaxes(small[:, :, experts : experts + 2], 1, 2),
        jnp.swapaxes(small[:, :, experts + 2 : experts + 5], 1, 2),
        jnp.stack([parts[0][None] for parts in expert_grads]),
        jnp.stack([parts[2] for parts in expert_grads]),
        jnp.stack([parts[1][None] for parts in expert_grads]),
        jnp.stack([parts[3] for parts in expert_grads]),
    )


def solution(mesh):
    tokens = P(("rep", "exp"), None)
    placed = (
        tokens,
        P(None, ("rep", "exp"), None),
        P(None, ("rep", "exp"), None, "mdl"),
        P(None, "mdl", ("rep", "exp")),
        P(None, ("rep", "exp"), None),
        P(None, None, ("rep", "exp")),
        P(None, None, ("rep", "exp")),
        P(None, "exp", "rep", "mdl"),
        P(None, "exp", "mdl"),
        P(None, "exp", "mdl", "rep"),
        P(None, "exp", "rep"),
    )
    return jax.shard_map(
        on_device,
        mesh=mesh,
        in_specs=placed + (tokens,),
        out_specs=(tokens, tokens) + placed[2:],
        check_vma=False,
    )
```

profile of v0, /device:TPU:0, one launch (start us, length us, event | category | flops | bytes accessed | tf_op | source)
XLA Modules:
  0.0 352.8 jit_solution(7938206067796578169)
XLA Ops:
  0.7 1.9 slice_bitcast_fusion.1
  3.1 1.3 slice_bitcast_fusion
  5.8 0.7 fusion.12.hot0
  6.5 0.7 fusion.13.hot1
  7.7 0.7 fusion.14.hot0
  8.4 0.7 fusion.15.hot1
  9.2 0.8 fusion.3.turned0
  9.9 0.8 fusion.16.turned
  10.8 0.8 fusion.4.turned1
  11.5 0.8 fusion.7.pick0
  12.3 0.8 fusion.8.pick1
  13.1 0.8 fusion.18.pick
  13.9 0.8 fusion.1.turned0
  14.7 0.8 fusion.17.turned
  15.6 0.8 fusion.2.turned1
  16.4 0.8 fusion.5.pick0
  17.2 0.8 fusion.6.pick1
  17.9 0.8 fusion.19.pick
  18.8 1.5 fusion.spread
  20.2 0.9 pad_convert_fusion.1.state.state_in
  21.1 0.6 slice_bitcast_fusion.6
  21.7 0.9 pad_convert_fusion.grad_state
  22.6 1.4 copy.37
  24.1 1.3 copy.48
  25.4 0.8 copy.35
  26.2 1.4 copy.36
  28.2 1.6 concatenate.15
  29.8 1.6 pad.25.mine
  31.3 36.6 %gather_weights.1 = (bf16[2,32,16,1664]{3,2,1,0:T(8,128)(2,1)}, bf16[2,32,16,1664]{3,2,1,0:T(8,128)(2,1)}) custom-call(bf16[2,16,1664]{2,1,0:T(8,128)(2,1)} %pad.25.mine), custom_call_target="tpu_custom_call" | custom-call | tf_op jit(solution)/shard_map/gather_weights/pallas_call | solution.py:188
  67.9 0.7 broadcast_select_fusion.1
  69.2 52.7 %block_forward.2 = (f32[208,768]{1,0:T(8,128)}, bf16[208,768]{1,0:T(8,128)(2,1)}, f32[208,128]{1,0:T(8,128)}, bf16[208,768]{1,0:T(8,128)(2,1)}, bf16[208,768]{1,...) custom-call(f32[208,768]{1,0:T(8,128)} %pad_convert_fusion.1.state.s, ...), custom_call_target="tpu_custom_call" | custom-call | tf_op jit(solution)/shard_map/block_forward/pallas_call | solution.py:711
  121.9 48.1 %block_forward.3 = (f32[208,768]{1,0:T(8,128)}, bf16[208,768]{1,0:T(8,128)(2,1)}, f32[208,128]{1,0:T(8,128)}, bf16[208,768]{1,0:T(8,128)(2,1)}, bf16[208,768]{1,...) custom-call(f32[208,768]{1,0:T(8,128)} %get-tuple-element.58.state.s, ...), custom_call_target="tpu_custom_call" | custom-call | tf_op jit(solution)/shard_map/block_forward/pallas_call | solution.py:711
  170.1 52.9 %block_backward.2 = (f32[208,768]{1,0:T(8,128)}, bf16[208,768]{1,0:T(8,128)(2,1)}, bf16[208,128]{1,0:T(8,128)(2,1)}, f32[128,768]{1,0:T(8,128)}, bf16[208,1152]{...) custom-call(f32[208,768]{1,0:T(8,128)} %pad_convert_fusion.grad_state, ...), custom_call_target="tpu_custom_call" | custom-call | tf_op jit(solution)/shard_map/block_backward/pallas_call | solution.py:975
  223.0 54.6 %block_backward.3 = (f32[208,768]{1,0:T(8,128)}, bf16[208,768]{1,0:T(8,128)(2,1)}, bf16[208,128]{1,0:T(8,128)(2,1)}, f32[128,768]{1,0:T(8,128)}, bf16[208,1152]{...) custom-call(f32[208,768]{1,0:T(8,128)} %get-tuple-element.71.grad_state, ...), custom_call_target="tpu_custom_call" | custom-call | tf_op jit(solution)/shard_map/block_backward/pallas_call | solution.py:975
  277.6 1.1 copy-done.4
  278.7 1.0 copy-done.6
  279.7 1.0 copy-done.12
  280.7 0.8 copy-done.14
  281.5 27.9 %scatter_grads.2 = f32[16,1664]{1,0:T(8,128)S(1)} custom-call(bf16[208,768]{1,0:T(8,128)(2,1)S(1)} %copy-done.8, bf16[208,768]{1,0:T(8,128)(2,1)S(1)} %copy-done.12, bf16[208,768]{1,0:T(8,128)(2,1)S(1)} %copy-done.7, bf16[208,1152]{1,0:T(8,128)(2,1)S(1)} %copy-done.4, bf16[208,384]{1,0:T(8,128)(2,1)S(1)} %copy-done.1, bf16[208,128]{1,0:T(8,128)(2,1)S(1)} %copy-done.14, ...), custom_call_target="tpu_custom_call" | custom-call | tf_op jit(solution)/shard_map/scatter_grads/pallas_call | solution.py:350
  309.5 28.6 %scatter_grads.3 = f32[16,1664]{1,0:T(8,128)S(1)} custom-call(bf16[208,768]{1,0:T(8,128)(2,1)S(1)} %copy-done.10, bf16[208,768]{1,0:T(8,128)(2,1)S(1)} %copy-done.11, bf16[208,768]{1,0:T(8,128)(2,1)S(1)} %copy-done.9, bf16[208,1152]{1,0:T(8,128)(2,1)S(1)} %copy-done.3, bf16[208,384]{1,0:T(8,128)(2,1)S(1)} %copy-done.2, bf16[208,128]{1,0:T(8,128)(2,1)S(1)} %copy-done.13, ...), custom_call_target="tpu_custom_call" | custom-call | tf_op jit(solution)/shard_map/scatter_grads/pallas_call | solution.py:350
  338.4 1.9 slice.165
  340.3 0.9 slice.93
  341.2 0.7 copy.40
  341.9 0.6 copy.41
  343.2 0.7 copy.43
  343.9 0.7 copy.44
  344.5 4.3 %pad_maximum_fusion = f32[2,1,384,1536]{3,2,1,0:T(8,128)} fusion(f32[1,1,384,1536]{3,2,1,0:T(8,128)S(1)} %bitcast.63, f32[1,1,384,1536]{3,2,1,0:T(8,128)} %bitcast.65), kind=kLoop, calls=%fused_computation | loop fusion | flops 1179648 | bytes 9437184 | tf_op jit(solution)/shard_map/stack | solution.py:1180
  349.5 2.5 pad_maximum_fusion.1
  (100 shorter events, 5.6 us)
Async XLA Ops:
  0.6 2.5 copy-start.18
  0.7 67.3 %collective-permute-start = (bf16[2,1,384]{2,0,1:T(2,128)(2,1)}, bf16[2,1,384]{2,0,1:T(2,128)(2,1)}, u32[]{:S(2)}, u32[]{:S(2)}) collective-permute-start(bf16[2,1,384]{2,0,1:T(2,128)(2,1)} %param.22), channel_id=1, source_target_pairs={{0,64},{64,0},{1,65},{65,1},{2,66},{66,2},{3,67},{67,3},{4,68},{68... | collective-permute-start | bytes 4616 | tf_op jit(solution)/shard_map/ppermute | solution.py:35
  2.7 1.8 copy-start.15
  2.7 2.1 copy-start.17
  2.7 2.7 copy-start.29
  2.7 66.5 %collective-permute-start.1 = (bf16[384,1536]{1,0:T(8,128)(2,1)S(1)}, bf16[384,1536]{1,0:T(8,128)(2,1)}, u32[]{:S(2)}, u32[]{:S(2)}) collective-permute-start(bf16[384,1536]{1,0:T(8,128)(2,1)S(1)} %get-tuple-element.132.own_in), channel_id=1, source_target_pairs={{0,64},{64,0},{1,65},{65,1},{2,66},{66,2},{3,67},{67,3},{4,68},{68... | collective-permute-start | bytes 3538952 | tf_op jit(solution)/shard_map/ppermute | solution.py:35
  4.5 15.7 %copy-start.16 = (bf16[1536,384]{1,0:T(8,128)(2,1)}, bf16[1536,384]{1,0:T(8,128)(2,1)S(1)}, u32[]{:S(2)}) copy-start(bf16[1536,384]{1,0:T(8,128)(2,1)S(1)} %get-tuple-element.130.own_out) | copy-start | bytes 3538948
  4.5 64.7 %collective-permute-start.2 = (bf16[1536,384]{1,0:T(8,128)(2,1)S(1)}, bf16[1536,384]{1,0:T(8,128)(2,1)}, u32[]{:S(2)}, u32[]{:S(2)}) collective-permute-start(bf16[1536,384]{1,0:T(8,128)(2,1)S(1)} %get-tuple-element.130.own_out), channel_id=1, source_target_pairs={{0,64},{64,0},{1,65},{65,1},{2,66},{66,2},{3,67},{67,3},{4,68},{68... | collective-permute-start | bytes 3538952 | tf_op jit(solution)/shard_map/ppermute | solution.py:35
  4.8 117.1 %collective-permute-start.3 = (bf16[384,1536]{1,0:T(8,128)(2,1)S(1)}, bf16[384,1536]{1,0:T(8,128)(2,1)}, u32[]{:S(2)}, u32[]{:S(2)}) collective-permute-start(bf16[384,1536]{1,0:T(8,128)(2,1)S(1)} %get-tuple-element.131.own_in), channel_id=1, source_target_pairs={{0,64},{64,0},{1,65},{65,1},{2,66},{66,2},{3,67},{67,3},{4,68},{68... | collective-permute-start | bytes 3538952 | tf_op jit(solution)/shard_map/ppermute | solution.py:35
  5.0 116.9 %collective-permute-start.4 = (bf16[1536,384]{1,0:T(8,128)(2,1)}, bf16[1536,384]{1,0:T(8,128)(2,1)}, u32[]{:S(2)}, u32[]{:S(2)}) collective-permute-start(bf16[1536,384]{1,0:T(8,128)(2,1)} %get-tuple-element.129.own_out), channel_id=1, source_target_pairs={{0,64},{64,0},{1,65},{65,1},{2,66},{66,2},{3,67},{67,3},{4,68},{68... | collective-permute-start | bytes 3538952 | tf_op jit(solution)/shard_map/ppermute | solution.py:35
  7.7 12.6 %copy-start.23 = (bf16[197,768]{1,0:T(8,128)(2,1)S(1)}, bf16[197,768]{1,0:T(8,128)(2,1)}, u32[]{:S(2)}) copy-start(bf16[197,768]{1,0:T(8,128)(2,1)} %param.12) | copy-start | bytes 907780
  11.5 9.6 %copy-start.25 = (bf16[2,1,1536]{2,0,1:T(2,128)(2,1)S(1)}, bf16[2,1,1536]{2,0,1:T(2,128)(2,1)}, u32[]{:S(2)}) copy-start(bf16[2,1,1536]{2,0,1:T(2,128)(2,1)} %param.20) | copy-start | bytes 18436
  11.5 10.2 %copy-start.24 = (bf16[197,768]{1,0:T(8,128)(2,1)S(1)}, bf16[197,768]{1,0:T(8,128)(2,1)}, u32[]{:S(2)}) copy-start(bf16[197,768]{1,0:T(8,128)(2,1)} %param.23) | copy-start | bytes 907780
  15.6 9.8 %copy-start.26 = (bf16[2,12,32]{2,0,1:T(2,128)(2,1)S(1)}, bf16[2,12,32]{2,0,1:T(2,128)(2,1)}, u32[]{:S(2)}) copy-start(bf16[2,12,32]{2,0,1:T(2,128)(2,1)} %param.16) | copy-start | bytes 4612
  222.9 54.7 %copy-start = (bf16[1024,768]{1,0:T(8,128)(2,1)S(1)}, bf16[1024,768]{1,0:T(8,128)(2,1)}, u32[]{:S(2)}) copy-start(bf16[1024,768]{1,0:T(8,128)(2,1)} %fusion.spread) | copy-start | bytes 4718596
  222.9 54.7 %copy-start.1 = (bf16[208,384]{1,0:T(8,128)(2,1)S(1)}, bf16[208,384]{1,0:T(8,128)(2,1)}, u32[]{:S(2)}) copy-start(bf16[208,384]{1,0:T(8,128)(2,1)} %get-tuple-element.78.heads.rhs_proj) | copy-start | bytes 479236
  222.9 54.7 %copy-start.7 = (bf16[208,768]{1,0:T(8,128)(2,1)S(1)}, bf16[208,768]{1,0:T(8,128)(2,1)}, u32[]{:S(2)}) copy-start(bf16[208,768]{1,0:T(8,128)(2,1)} %get-tuple-element.85.h_two) | copy-start | bytes 958468
  222.9 54.7 %copy-start.8 = (bf16[208,768]{1,0:T(8,128)(2,1)S(1)}, bf16[208,768]{1,0:T(8,128)(2,1)}, u32[]{:S(2)}) copy-start(bf16[208,768]{1,0:T(8,128)(2,1)} %get-tuple-element.83.h_one) | copy-start | bytes 958468
  223.0 86.5 %copy-start.5 = (f32[128,768]{1,0:T(8,128)S(1)}, f32[128,768]{1,0:T(8,128)}, u32[]{:S(2)}) copy-start(f32[128,768]{1,0:T(8,128)} %get-tuple-element.94.sums_in) | copy-start | bytes 1179652
  223.0 86.5 %copy-start.9 = (bf16[208,768]{1,0:T(8,128)(2,1)S(1)}, bf16[208,768]{1,0:T(8,128)(2,1)}, u32[]{:S(2)}) copy-start(bf16[208,768]{1,0:T(8,128)(2,1)} %get-tuple-element.91.h_two) | copy-start | bytes 958468
  223.0 86.5 %copy-start.10 = (bf16[208,768]{1,0:T(8,128)(2,1)S(1)}, bf16[208,768]{1,0:T(8,128)(2,1)}, u32[]{:S(2)}) copy-start(bf16[208,768]{1,0:T(8,128)(2,1)} %get-tuple-element.89.h_one) | copy-start | bytes 958468
  223.0 86.5 %copy-start.11 = (bf16[208,768]{1,0:T(8,128)(2,1)S(1)}, bf16[208,768]{1,0:T(8,128)(2,1)}, u32[]{:S(2)}) copy-start(bf16[208,768]{1,0:T(8,128)(2,1)} %get-tuple-element.90.grad_attended) | copy-start | bytes 958468
  223.0 86.5 %copy-start.13 = (bf16[208,128]{1,0:T(8,128)(2,1)S(1)}, bf16[208,128]{1,0:T(8,128)(2,1)}, u32[]{:S(2)}) copy-start(bf16[208,128]{1,0:T(8,128)(2,1)} %get-tuple-element.93.rhs_small) | copy-start | bytes 159748
  277.6 31.9 %copy-start.2 = (bf16[208,384]{1,0:T(8,128)(2,1)S(1)}, bf16[208,384]{1,0:T(8,128)(2,1)}, u32[]{:S(2)}) copy-start(bf16[208,384]{1,0:T(8,128)(2,1)} %get-tuple-element.67.heads.rhs_proj) | copy-start | bytes 479236
  277.6 31.9 %copy-start.3 = (bf16[208,1152]{1,0:T(8,128)(2,1)S(1)}, bf16[208,1152]{1,0:T(8,128)(2,1)}, u32[]{:S(2)}) copy-start(bf16[208,1152]{1,0:T(8,128)(2,1)} %get-tuple-element.92.rhs_qkv) | copy-start | bytes 1437700
  277.6 1.1 copy-start.4
  278.7 1.0 copy-start.6
  279.7 1.0 copy-start.12
  280.7 0.8 copy-start.14
  309.5 30.8 %copy-start.22 = (f32[208,768]{1,0:T(8,128)S(1)}, f32[208,768]{1,0:T(8,128)}, u32[]{:S(2)}) copy-start(f32[208,768]{1,0:T(8,128)} %get-tuple-element.82) | copy-start | bytes 1916932
  338.2 6.4 %copy-start.20 = (f32[384,1536]{1,0:T(8,128)S(1)}, f32[384,1536]{1,0:T(8,128)}, u32[]{:S(2)}) copy-start(f32[384,1536]{1,0:T(8,128)} %get-tuple-element.96) | copy-start | bytes 7077892
  344.5 4.4 %copy-start.27 = (f32[1,1536]{1,0:T(1,128)S(1)}, f32[1,1536]{1,0:T(1,128)}, u32[]{:S(2)}) copy-start(f32[1,1536]{1,0:T(1,128)} %get-tuple-element.98) | copy-start | bytes 18436
  344.5 4.4 %copy-start.28 = (f32[1,1536]{1,0:T(1,128)S(1)}, f32[1,1536]{1,0:T(1,128)}, u32[]{:S(2)}) copy-start(f32[1,1536]{1,0:T(1,128)} %get-tuple-element.97) | copy-start | bytes 18436
  344.5 5.0 %copy-start.19 = (f32[1536,384]{1,0:T(8,128)S(1)}, f32[1536,384]{1,0:T(8,128)}, u32[]{:S(2)}) copy-start(f32[1536,384]{1,0:T(8,128)} %get-tuple-element.100) | copy-start | bytes 7077892
  344.5 5.0 %copy-start.21 = (f32[1536,384]{1,0:T(8,128)S(1)}, f32[1536,384]{1,0:T(8,128)}, u32[]{:S(2)}) copy-start(f32[1536,384]{1,0:T(8,128)} %get-tuple-element.99) | copy-start | bytes 7077892
  349.5 2.5 copy-start.30
  349.5 2.5 copy-start.31
where the time goes:
time: 358 us; the launch traced here: 353 us
  Pallas kernels  301 us (84%)
  other arithmetic  24.6 us (7%)
  local copies, waits for them, and re-layouts  23.3 us (7%)
    pallas_call x2, Pallas kernels, block_backward(): pl.pallas_call(block_backward_kernel, out_shape=(shape((tokens, width), F...  107 us
    pallas_call x2, Pallas kernels, block_forward(): pl.pallas_call(block_forward_kernel, out_shape=(shape((tokens, width), F3...  101 us
    pallas_call x2, Pallas kernels, scatter_grads(): pl.pallas_call(scatter_kernel, out_shape=jax.ShapeDtypeStruct((BLOCK, col...  56.5 us
    pallas_call x1, Pallas kernels, gather_weights(): pl.pallas_call(gather_kernel, out_shape=(whole, whole), in_specs=[pl.Bloc...  36.6 us
    unnamed x73, local copies, waits for them, and re-layouts  10.8 us
  transfers between devices with their start and end apart: 5, of which 0 were waited for; matrix products, arithmetic and copies ran while one was open for 9% of the time, Pallas kernels for 25%

commit v1 on v0

--- a/solution.py
+++ b/solution.py
@@ -44,6 +44,9 @@
 
 MESH = pl.DeviceIdType.MESH
 BLOCK = 16
+VMEM_SPEC = pl.BlockSpec(memory_space=pltpu.VMEM)
+ANY_SPEC = pl.BlockSpec(memory_space=pl.ANY)
+SMALL = 128
 NEAR = 8
 FAR = 4
 
@@ -71,13 +74,24 @@
         peer = chip_of(near, (far + step) % FAR)
         pl.semaphore_signal(barrier, inc=1, device_id={"exp": peer}, device_id_type=MESH)
     pl.semaphore_signal(barrier, inc=1, device_id={"rep": 1 - rep}, device_id_type=MESH)
-    pl.semaphore_wait(barrier, NEAR + FAR - 1)
+    return barrier
+
+
+GREETED = NEAR + FAR - 1
 
 
 def gather_kernel(
-    mine,
+    w_qkv,
+    w_out,
+    router,
+    gains,
+    shifts,
     whole0,
     whole1,
+    spread,
+    mine,
+    filled,
+    vectors,
     own_sem,
     near_send,
     near_recv,
@@ -123,15 +137,43 @@
         pltpu.make_async_copy(mine.at[layer], wholes[layer].at[rep, exp], own_sem.at[layer])
         for layer in range(2)
     ]
+    barrier = greet(near, far, chip_of, rep)
+    layers, own_rows, parts, part_cols = w_qkv.shape
+    qkv_cols = parts * part_cols
+    cut = qkv_cols + w_out.shape[1]
+    experts = router.shape[2]
+    turn = (
+        lax.broadcasted_iota(jnp.int32, (BLOCK, own_rows), 0)
+        == lax.broadcasted_iota(jnp.int32, (BLOCK, own_rows), 1)
+    )
+    turn = jnp.where(turn, 1.0, 0.0).astype(BF16)
+    filled[...] = jnp.zeros_like(filled)
+    vectors[...] = jnp.zeros_like(vectors)
+    for layer in range(layers):
+        for part in range(parts):
+            filled[:own_rows, part * part_cols : (part + 1) * part_cols] = w_qkv[
+                layer, :, part, :
+            ].astype(F32)
+        filled[:, qkv_cols:cut] = dot_nt(turn, w_out[layer])
+        vectors[experts : experts + 2, :] = gains[layer].astype(F32)
+        vectors[experts + 2 : experts + 5, :] = shifts[layer].astype(F32)
+        filled[:, cut:] = dot_nt(turn, vectors[...].astype(BF16))
+        filled[:own_rows, cut : cut + experts] = router[layer].astype(F32)
+        mine[layer] = filled[...].astype(BF16)
     for keep in keeps:
         keep.start()
-    greet(near, far, chip_of, rep)
+    pl.semaphore_wait(barrier, GREETED)
     for layer in range(2):
 
         @pl.loop(1, NEAR)
         def _(step):
             near_copy(layer, step, near).start()
 
+    row = lax.broadcasted_iota(jnp.int32, spread.shape, 0)
+    col = lax.broadcasted_iota(jnp.int32, spread.shape, 1)
+    inside = row & (BLOCK - 1)
+    true_row = (row >> 4) * own_rows + inside
+    spread[...] = jnp.where((inside < own_rows) & (true_row == col), 1.0, 0.0).astype(BF16)
     for keep in keeps:
         keep.wait()
     for layer in range(2):
@@ -182,15 +224,24 @@
                 far_copy(layer, step, chip_of(slot, far), slot, far).wait_send()
 
 
-def gather_weights(packed):
-    layers, rows, cols = packed.shape
-    whole = jax.ShapeDtypeStruct((2, NEAR * FAR, rows, cols), BF16)
+def gather_weights(w_qkv, w_out, router, gains, shifts):
+    layers, own_rows, parts, part_cols = w_qkv.shape
+    cols = parts * part_cols + w_out.shape[1] + SMALL
+    devices = 2 * NEAR * FAR
+    whole = jax.ShapeDtypeStruct((2, NEAR * FAR, BLOCK, cols), BF16)
     got = pl.pallas_call(
         gather_kernel,
-        out_shape=(whole, whole),
-        in_specs=[pl.BlockSpec(memory_space=pl.ANY)],
-        out_specs=(pl.BlockSpec(memory_space=pl.ANY), pl.BlockSpec(memory_space=pl.ANY)),
+        out_shape=(
+            whole,
+            whole,
+            jax.ShapeDtypeStruct((devices * BLOCK, devices * own_rows), BF16),
+        ),
+        in_specs=[VMEM_SPEC] * 5,
+        out_specs=(ANY_SPEC, ANY_SPEC, VMEM_SPEC),
         scratch_shapes=[
+            pltpu.VMEM((layers, BLOCK, cols), BF16),
+            pltpu.VMEM((BLOCK, cols), F32),
+            pltpu.VMEM((SMALL, own_rows), F32),
             pltpu.SemaphoreType.DMA((2,)),
             pltpu.SemaphoreType.DMA((2, NEAR)),
             pltpu.SemaphoreType.DMA((2, NEAR)),
@@ -199,181 +250,240 @@
             pltpu.SemaphoreType.DMA((2, NEAR * FAR)),
             pltpu.SemaphoreType.DMA((2, NEAR * FAR)),
         ],
-        compiler_params=pltpu.CompilerParams(collective_id=0, has_side_effects=True),
+        compiler_params=pltpu.CompilerParams(
+            collective_id=0, has_side_effects=True, vmem_limit_bytes=32 << 20
+        ),
         name="gather_weights",
-    )(packed)
-    return [value.reshape(2 * NEAR * FAR * rows, cols) for value in got]
-
-
-def scatter_kernel(
-    h_one,
-    grad_attended,
-    h_two,
-    rhs_qkv,
-    rhs_proj,
-    rhs_small,
-    sums_in,
-    spread,
-    out,
-    lhs_qkv,
-    lhs_proj,
-    lhs_small,
-    sums,
-    part,
-    from_core,
-    from_far,
-    total,
-    from_near,
-    core_send,
-    core_recv,
-    far_send,
-    far_recv,
-    near_send,
-    near_recv,
-):
+    )(w_qkv, w_out, router, gains, shifts)
+    return [value.reshape(devices * BLOCK, cols) for value in got[:2]], got[2]
+
+
+def scatter_kernel(*refs):
+    per_layer = [refs[7 * layer : 7 * layer + 7] for layer in range(2)]
+    spread = refs[14]
+    biases = refs[15:19]
+    experts = refs[19:23]
+    out_qkv, out_rest, out_b_in, out_b_out, out_in, out_exp = refs[23:29]
+    (
+        lhs_qkv,
+        lhs_proj,
+        lhs_small,
+        sums,
+        part,
+        from_core,
+        from_far,
+        total,
+        from_near,
+        stage_in,
+        stage_exp,
+        stage_sems,
+        core_send,
+        core_recv,
+        far_send,
+        far_recv,
+        near_send,
+        near_recv,
+    ) = refs[29:]
     rep, exp, near, far, chip_of = chip_place()
-    qkv_cols, proj_cols = rhs_qkv.shape[1], rhs_proj.shape[1]
+    qkv_cols, proj_cols = per_layer[0][3].shape[1], per_layer[0][4].shape[1]
     cut = qkv_cols + proj_cols
-    rows = BLOCK * 4
-    chunks = NEAR * FAR // 4
-
-    def multiply(core, chunk):
+    rows = BLOCK * 8
+    chunks = NEAR * FAR // 8
+    loads, stores = [], []
+    for layer in range(2):
+        for kind, (stage, out) in enumerate(((stage_in, out_in), (stage_exp, out_exp))):
+            idx = 2 * layer + kind
+            loads.append(
+                pltpu.make_async_copy(experts[idx], stage.at[layer], stage_sems.at[idx])
+            )
+            stores.append(
+                pltpu.make_async_copy(stage.at[layer], out.at[layer, 0], stage_sems.at[idx])
+            )
+    for load in loads:
+        load.start()
+
+    def multiply(layer, core, chunk):
+        rhs_qkv, rhs_proj, rhs_small = per_layer[layer][3:6]
         at = pl.ds(pl.multiple_of((core * chunks + chunk) * rows, rows), rows)
         to = pl.ds(pl.multiple_of(chunk * rows, rows), rows)
-        low = lambda lhs, rhs: jnp.dot(
-            lhs[at, :], rhs[...], preferred_element_type=F32
-        )
-        part[core, to, :qkv_cols] = low(lhs_qkv, rhs_qkv).astype(BF16)
-        part[core, to, qkv_cols:cut] = low(lhs_proj, rhs_proj).astype(BF16)
-        part[core, to, cut:] = (low(lhs_small, rhs_small) + sums[at, :]).astype(BF16)
-
-    def core_copy(chunk):
+        part[layer, core, to, :qkv_cols] = dot(lhs_qkv[at, :], rhs_qkv[...]).astype(BF16)
+        part[layer, core, to, qkv_cols:cut] = dot(lhs_proj[at, :], rhs_proj[...]).astype(BF16)
+        part[layer, core, to, cut:] = (
+            dot(lhs_small[at, :], rhs_small[...]) + sums[at, :]
+        ).astype(BF16)
+
+    def core_copy(layer, chunk):
         to = pl.ds(pl.multiple_of(chunk * rows, rows), rows)
         return pltpu.make_async_remote_copy(
-            src_ref=part.at[1 - rep, to],
-            dst_ref=from_core.at[to],
-            send_sem=core_send.at[chunk],
-            recv_sem=core_recv.at[chunk],
+            src_ref=part.at[layer, 1 - rep, to],
+            dst_ref=from_core.at[layer, to],
+            send_sem=core_send.at[layer, chunk],
+            recv_sem=core_recv.at[layer, chunk],
             device_id={"rep": 1 - rep},
             device_id_type=MESH,
         )
 
-    def far_copy(step, slot):
+    def far_copy(layer, step, slot):
         return pltpu.make_async_remote_copy(
-            src_ref=part.at[rep, block(chip_of(slot, (far + step) % FAR))],
-            dst_ref=from_far.at[step, block(slot)],
-            send_sem=far_send.at[step, slot],
-            recv_sem=far_recv.at[step, slot],
+            src_ref=part.at[layer, rep, block(chip_of(slot, (far + step) % FAR))],
+            dst_ref=from_far.at[layer, step, block(slot)],
+            send_sem=far_send.at[layer, step, slot],
+            recv_sem=far_recv.at[layer, step, slot],
             device_id={"exp": chip_of(near, (far + step) % FAR)},
             device_id_type=MESH,
         )
 
-    def near_copy(step):
+    def near_copy(layer, step):
         return pltpu.make_async_remote_copy(
-            src_ref=total.at[block((near + step) % NEAR)],
-            dst_ref=from_near.at[step],
-            send_sem=near_send.at[step],
-            recv_sem=near_recv.at[step],
+            src_ref=total.at[layer, block((near + step) % NEAR)],
+            dst_ref=from_near.at[layer, step],
+            send_sem=near_send.at[layer, step],
+            recv_sem=near_recv.at[layer, step],
             device_id={"exp": chip_of((near + step) % NEAR, far)},
             device_id_type=MESH,
         )
 
-    lhs_qkv[...] = dot_nt(spread[...], h_one[...]).astype(BF16)
-    lhs_proj[...] = dot_nt(spread[...], grad_attended[...]).astype(BF16)
-    lhs_small[...] = dot_nt(spread[...], h_two[...]).astype(BF16)
-    sums[...] = dot_nt(spread[...], sums_in[...].astype(BF16))
-    greet(near, far, chip_of, rep)
-
-    @pl.loop(0, chunks)
-    def _(chunk):
-        multiply(1 - rep, chunk)
-        core_copy(chunk).start()
-
-    @pl.loop(0, chunks)
-    def _(chunk):
-        multiply(rep, chunk)
-
-    @pl.loop(0, chunks)
-    def _(chunk):
-        to = pl.ds(pl.multiple_of(chunk * rows, rows), rows)
-        core_copy(chunk).wait_recv()
-        part[rep, to, :] = (
-            part[rep, to, :].astype(F32) + from_core[to, :].astype(F32)
-        ).astype(BF16)
-
-    @pl.loop(1, FAR)
-    def _(step):
+    barrier = greet(near, far, chip_of, rep)
+    for layer in range(2):
+        h_one, grad_att, h_two = per_layer[layer][:3]
+        lhs_qkv[...] = dot_nt(spread[...], h_one[...]).astype(BF16)
+        lhs_proj[...] = dot_nt(spread[...], grad_att[...]).astype(BF16)
+        lhs_small[...] = dot_nt(spread[...], h_two[...]).astype(BF16)
+        sums[...] = dot_nt(spread[...], per_layer[layer][6][...].astype(BF16))
+        if layer == 0:
+            pl.semaphore_wait(barrier, GREETED)
+
+        @pl.loop(0, chunks)
+        def _(chunk):
+            multiply(layer, 1 - rep, chunk)
+            core_copy(layer, chunk).start()
+
+        @pl.loop(0, chunks)
+        def _(chunk):
+            multiply(layer, rep, chunk)
+
+    for layer in range(2):
+
+        @pl.loop(0, chunks)
+        def _(chunk):
+            to = pl.ds(pl.multiple_of(chunk * rows, rows), rows)
+            core_copy(layer, chunk).wait_recv()
+            part[layer, rep, to, :] = (
+                part[layer, rep, to, :].astype(F32) + from_core[layer, to, :].astype(F32)
+            ).astype(BF16)
+
         @pl.loop(1, NEAR + 1)
         def _(ahead):
-            far_copy(step, (near + ahead) % NEAR).start()
-
-    def add_far(slot):
+            @pl.loop(1, FAR)
+            def _(step):
+                far_copy(layer, step, (near + ahead) % NEAR).start()
+
+    for load in loads:
+        load.wait()
+    for store in stores:
+        store.start()
+    for layer in range(2):
+        out_b_in[layer] = biases[2 * layer][...]
+        out_b_out[layer] = biases[2 * layer + 1][...]
+
+    def add_far(layer, slot):
         for step in range(1, FAR):
-            far_copy(step, slot).wait_recv()
-        value = part[rep, block(chip_of(slot, far)), :].astype(F32)
+            far_copy(layer, step, slot).wait_recv()
+        value = part[layer, rep, block(chip_of(slot, far)), :].astype(F32)
         for step in range(1, FAR):
-            value = value + from_far[step, block(slot), :].astype(F32)
+            value = value + from_far[layer, step, block(slot), :].astype(F32)
         return value
 
-    @pl.loop(1, NEAR)
-    def _(step):
-        slot = (near + step) % NEAR
-        total[block(slot), :] = add_far(slot).astype(BF16)
-        near_copy(step).start()
-
-    out[...] = add_far(near)
-
-    @pl.loop(1, NEAR)
-    def _(step):
-        near_copy(step).wait_recv()
-        out[...] += from_near[step].astype(F32)
-
-    @pl.loop(1, NEAR)
-    def _(step):
-        near_copy(step).wait_send()
-
-    @pl.loop(1, FAR)
-    def _(step):
-        @pl.loop(0, NEAR)
-        def _(slot):
-            far_copy(step, slot).wait_send()
-
-    @pl.loop(0, chunks)
-    def _(chunk):
-        core_copy(chunk).wait_send()
-
-
-def scatter_grads(lhs, rhs, sums, spread):
-    cols = sum(r.shape[1] for r in rhs)
+    for layer in range(2):
+
+        @pl.loop(1, NEAR)
+        def _(step):
+            slot = (near + step) % NEAR
+            total[layer, block(slot), :] = add_far(layer, slot).astype(BF16)
+            near_copy(layer, step).start()
+
+    own_rows = out_qkv.shape[1]
+    part_cols = qkv_cols // 3
+    for layer in range(2):
+        value = add_far(layer, near)
+        for step in range(1, NEAR):
+            near_copy(layer, step).wait_recv()
+            value = value + from_near[layer, step].astype(F32)
+        for idx in range(3):
+            out_qkv[layer, :, idx, :] = value[:own_rows, idx * part_cols : (idx + 1) * part_cols]
+        out_rest[layer] = value[:, qkv_cols:]
+
+    for layer in range(2):
+
+        @pl.loop(1, NEAR)
+        def _(step):
+            near_copy(layer, step).wait_send()
+
+        @pl.loop(1, FAR)
+        def _(step):
+            @pl.loop(0, NEAR)
+            def _(slot):
+                far_copy(layer, step, slot).wait_send()
+
+        @pl.loop(0, chunks)
+        def _(chunk):
+            core_copy(layer, chunk).wait_send()
+
+    for store in stores:
+        store.wait()
+
+
+def scatter_grads(attn, spread, experts, own_rows):
+    tokens = attn[0][0].shape[0]
+    qkv_cols, proj_cols = attn[0][3].shape[1], attn[0][4].shape[1]
+    cols = qkv_cols + proj_cols + SMALL
     half = NEAR * FAR * BLOCK
-    tokens = lhs[0].shape[0]
+    grad_in, grad_exp, grad_b_in, grad_b_out = experts[0]
+    shape = jax.ShapeDtypeStruct
+    chunks = NEAR * FAR // 8
     return pl.pallas_call(
         scatter_kernel,
-        out_shape=jax.ShapeDtypeStruct((BLOCK, cols), F32),
-        in_specs=[pl.BlockSpec(memory_space=pltpu.VMEM)] * 8,
-        out_specs=pl.BlockSpec(memory_space=pltpu.VMEM),
+        out_shape=(
+            shape((2, own_rows, 3, qkv_cols // 3), F32),
+            shape((2, BLOCK, proj_cols + SMALL), F32),
+            shape((2,) + grad_b_in.shape, F32),
+            shape((2,) + grad_b_out.shape, F32),
+            shape((2, 1) + grad_in.shape, F32),
+            shape((2, 1) + grad_exp.shape, F32),
+        ),
+        in_specs=[VMEM_SPEC] * 19 + [ANY_SPEC] * 4,
+        out_specs=tuple([VMEM_SPEC] * 4 + [ANY_SPEC] * 2),
         scratch_shapes=[
             pltpu.VMEM((2 * half, tokens), BF16),
             pltpu.VMEM((2 * half, tokens), BF16),
             pltpu.VMEM((2 * half, tokens), BF16),
-            pltpu.VMEM((2 * half, 128), F32),
+            pltpu.VMEM((2 * half, SMALL), F32),
+            pltpu.VMEM((2, 2, half, cols), BF16),
             pltpu.VMEM((2, half, cols), BF16),
-            pltpu.VMEM((half, cols), BF16),
-            pltpu.VMEM((FAR, NEAR * BLOCK, cols), BF16),
-            pltpu.VMEM((NEAR * BLOCK, cols), BF16),
-            pltpu.VMEM((NEAR, BLOCK, cols), BF16),
-            pltpu.SemaphoreType.DMA((half // BLOCK // 4,)),
-            pltpu.SemaphoreType.DMA((half // BLOCK // 4,)),
-            pltpu.SemaphoreType.DMA((FAR, NEAR)),
-            pltpu.SemaphoreType.DMA((FAR, NEAR)),
-            pltpu.SemaphoreType.DMA((NEAR,)),
-            pltpu.SemaphoreType.DMA((NEAR,)),
+            pltpu.VMEM((2, FAR, NEAR * BLOCK, cols), BF16),
+            pltpu.VMEM((2, NEAR * BLOCK, cols), BF16),
+            pltpu.VMEM((2, NEAR, BLOCK, cols), BF16),
+            pltpu.VMEM((2,) + grad_in.shape, F32),
+            pltpu.VMEM((2,) + grad_exp.shape, F32),
+            pltpu.SemaphoreType.DMA((4,)),
+            pltpu.SemaphoreType.DMA((2, chunks)),
+            pltpu.SemaphoreType.DMA((2, chunks)),
+            pltpu.SemaphoreType.DMA((2, FAR, NEAR)),
+            pltpu.SemaphoreType.DMA((2, FAR, NEAR)),
+            pltpu.SemaphoreType.DMA((2, NEAR)),
+            pltpu.SemaphoreType.DMA((2, NEAR)),
         ],
         compiler_params=pltpu.CompilerParams(
-            collective_id=1, has_side_effects=True, vmem_limit_bytes=40 << 20
+            collective_id=1, has_side_effects=True, vmem_limit_bytes=56 << 20
         ),
         name="scatter_grads",
-    )(*lhs, *rhs, sums, spread)
+    )(
+        *attn[0],
+        *attn[1],
+        spread,
+        *(value for parts in experts for value in parts[2:]),
+        *(value for parts in experts for value in parts[:2]),
+    )
 
 
 PLANES = 4
@@ -517,11 +627,6 @@
     return total
 
 
-VMEM_SPEC = pl.BlockSpec(memory_space=pltpu.VMEM)
-ANY_SPEC = pl.BlockSpec(memory_space=pl.ANY)
-SMALL = 128
-
-
 def row_sems():
     return [pltpu.SemaphoreType.DMA((PLANES * PLANE,))] * 4
 
@@ -535,6 +640,22 @@
     scores = dot_nt(query_rows, key_rows) * HD ** (-0.5)
     col = lax.broadcasted_iota(jnp.int32, scores.shape, 1)
     return jnp.where(col < SEQ, scores, -1e30)
+
+
+def route(ids, hot0, hot1, pick0, pick1):
+    tokens, slots = pick0.shape
+    lane = lax.broadcasted_iota(jnp.int32, (tokens, 128), 1)
+    hots = [jnp.where(ids[:, k : k + 1] == lane, 1.0, 0.0) for k in range(2)]
+    hot0[...], hot1[...] = hots[0].astype(BF16), hots[1].astype(BF16)
+    row = lax.broadcasted_iota(jnp.int32, (tokens, tokens), 0)
+    col = lax.broadcasted_iota(jnp.int32, (tokens, tokens), 1)
+    before = jnp.where(row > col, 1.0, 0.0).astype(BF16)
+    earlier = dot(before, (hots[0] + hots[1]).astype(BF16))
+    place = lax.broadcasted_iota(jnp.int32, (tokens, slots), 1).astype(F32)
+    for k, pick in enumerate((pick0, pick1)):
+        within = jnp.sum(earlier * hots[k], axis=1, keepdims=True)
+        slot = ids[:, k : k + 1].astype(F32) * BLOCK + within
+        pick[...] = jnp.where(slot == place, 1.0, 0.0).astype(BF16)
 
 
 def attend_forward(qkv, heads, log_total):
@@ -570,11 +691,7 @@
 def block_forward_kernel(
     state,
     spread,
-    turned,
-    pick0,
-    pick1,
-    hot0,
-    hot1,
+    ids,
     b_in,
     b_out,
     whole_in,
@@ -595,6 +712,10 @@
     rows_out,
     slope_out,
     active_out,
+    hot0,
+    hot1,
+    pick0,
+    pick1,
     whole,
     w_in,
     w_out,
@@ -641,6 +762,7 @@
     wide = dot_nt(h_one, spread[...]).astype(BF16)
     qkv_out[...] = dot(wide, whole[:, :qkv_cols]).astype(BF16)
     attend_forward(qkv_out, heads_out, log_out)
+    route(ids, hot0, hot1, pick0, pick1)
     own_att[...] = dot(
         dot_nt(heads_out[...], whole[:, qkv_cols:cut]).astype(BF16), spread[...]
     ).astype(BF16)
@@ -652,7 +774,7 @@
     after_out[...] = after
     h_two = norm_rows(after, gain1, shift1).astype(BF16)
     h_out[...] = h_two
-    send[...] = dot(turned[...], h_two).astype(BF16)
+    send[...] = dot_tn(pick0[...] + pick1[...], h_two).astype(BF16)
     send_all(send, rows, exp, send_sem, recv_sem)
     logits = dot_nt(h_two, small.astype(BF16))
     chosen = [jnp.sum(logits * hot[...].astype(F32), axis=1, keepdims=True) for hot in (hot0, hot1)]
@@ -703,7 +825,7 @@
 
 def block_forward(near, whole, weights):
     tokens, width = near[0].shape
-    slots = near[2].shape[0]
+    slots = BLOCK * PLANES * PLANE
     hidden = weights[0].shape[1]
     cols = whole.shape[1]
     proj = (cols - SMALL) // 4
@@ -725,9 +847,13 @@
             shape((slots, hidden), BF16),
             shape((slots, hidden), BF16),
         ),
-        in_specs=[VMEM_SPEC] * 9 + [ANY_SPEC] * 5,
+        in_specs=[VMEM_SPEC] * 5 + [ANY_SPEC] * 5,
         out_specs=tuple([VMEM_SPEC] * 10 + [ANY_SPEC] * 3),
         scratch_shapes=[
+            pltpu.VMEM((tokens, 128), BF16),
+            pltpu.VMEM((tokens, 128), BF16),
+            pltpu.VMEM((tokens, slots), BF16),
+            pltpu.VMEM((tokens, slots), BF16),
             pltpu.VMEM(whole.shape, BF16),
             pltpu.VMEM((width, hidden), BF16),
             pltpu.VMEM((hidden, width), BF16),
@@ -772,14 +898,10 @@
 def block_backward_kernel(
     grad_state,
     spread,
+    ids,
     gates,
     picked0,
     picked1,
-    turned0,
-    turned1,
-    pick,
-    hot0,
-    hot1,
     after,
     state_in,
     qkv,
@@ -802,6 +924,10 @@
     grad_exp_out,
     grad_b_in_out,
     grad_b_out_out,
+    hot0,
+    hot1,
+    pick0,
+    pick1,
     whole,
     w_in,
     w_out,
@@ -856,9 +982,10 @@
     pl.semaphore_signal(barrier, inc=1, device_id={"rep": 1 - rep}, device_id_type=MESH)
     grad = grad_state[...]
     gate0, gate1 = gates[:, 0:1], gates[:, 1:2]
+    route(ids, hot0, hot1, pick0, pick1)
     send[...] = (
-        dot(turned0[...], (gate0 * grad).astype(BF16))
-        + dot(turned1[...], (gate1 * grad).astype(BF16))
+        dot_tn(pick0[...], (gate0 * grad).astype(BF16))
+        + dot_tn(pick1[...], (gate1 * grad).astype(BF16))
     ).astype(BF16)
     pl.semaphore_wait(barrier, PLANES * PLANE + 1)
     send_all(send, rows, exp, send_sem, recv_sem)
@@ -919,7 +1046,7 @@
     from_router = dot(grad_logits, small.astype(BF16))
     unit, scale = norm_parts(after[...])
     wait_back(back_src, back, exp, sems)
-    own_h[...] = dot(pick[...], back[...]).astype(BF16)
+    own_h[...] = dot(pick0[...] + pick1[...], back[...]).astype(BF16)
     second = half_copy(own_h, low_h, half_sems, 1)
     second.start()
     in_copy.wait_recv()
@@ -966,7 +1093,7 @@
 
 def block_backward(near, whole, weights, kept):
     tokens, width = near[0].shape
-    slots = near[5].shape[0]
+    slots = BLOCK * PLANES * PLANE
     hidden = weights[0].shape[1]
     cols = whole.shape[1]
     proj = (cols - SMALL) // 4
@@ -985,9 +1112,13 @@
             shape((1, hidden), F32),
             shape((1, half), F32),
         ),
-        in_specs=[VMEM_SPEC] * 15 + [ANY_SPEC] * 8,
+        in_specs=[VMEM_SPEC] * 11 + [ANY_SPEC] * 8,
         out_specs=tuple([VMEM_SPEC] * 9),
         scratch_shapes=[
+            pltpu.VMEM((tokens, 128), BF16),
+            pltpu.VMEM((tokens, 128), BF16),
+            pltpu.VMEM((tokens, slots), BF16),
+            pltpu.VMEM((tokens, slots), BF16),
             pltpu.VMEM(whole.shape, BF16),
             pltpu.VMEM((width, hidden), BF16),
             pltpu.VMEM((hidden, width), BF16),
@@ -1039,77 +1170,27 @@
     cotangent,
 ):
     tok_rows, width = tokens_in.shape
-    exp_count = lax.axis_size("exp")
-    experts = w_in.shape[1] * exp_count
-    capacity = 2 * tok_rows // experts + 4
-    score_scale = HD ** (-0.5)
     layers = w_qkv.shape[0]
     own_rows = w_qkv.shape[1]
-    qkv_cols = 3 * w_qkv.shape[3]
     out_cols = w_out.shape[1]
-    small_cols = 128
-    slot_count = experts * capacity
-
-    packed = jnp.concatenate(
-        [
-            w_qkv.reshape(layers, own_rows, qkv_cols),
-            jnp.swapaxes(w_out, 1, 2),
-            router,
-            jnp.swapaxes(gains, 1, 2),
-            jnp.swapaxes(shifts, 1, 2),
-            jnp.zeros((layers, own_rows, small_cols - experts - 5), BF16),
-        ],
-        axis=2,
-    )
-    packed = jnp.pad(packed, ((0, 0), (0, BLOCK - own_rows), (0, 0)))
-    wholes = gather_weights(packed)
+    experts = w_in.shape[1] * lax.axis_size("exp")
+    wholes, spread = gather_weights(w_qkv, w_out, router, gains, shifts)
     expert_w = []
     for layer_idx in range(layers):
         own_in, own_out = w_in[layer_idx, 0], w_exp_out[layer_idx, 0]
         expert_w.append((own_in, other_core(own_in), own_out, other_core(own_out)))
-    padded = wholes[0].shape[0]
-    pad_row = jnp.arange(padded, dtype=jnp.int32)
-    true_row = jnp.where(
-        pad_row % BLOCK < own_rows, pad_row // BLOCK * own_rows + pad_row % BLOCK, -1
-    )
-    spread = (true_row[:, None] == jnp.arange(width, dtype=jnp.int32)).astype(BF16)
     out_bias = 0.5 * in_order(b_out, other_core(b_out), 2).astype(F32)
 
-    tokens_pad = -(-tok_rows // BLOCK) * BLOCK
-    spare = tokens_pad - tok_rows
-    expert_cols = jnp.arange(128, dtype=jnp.int32)
-    slot_cols = jnp.arange(slot_count, dtype=jnp.int32)
-    row_idx = jnp.arange(tokens_pad, dtype=jnp.int32)
-    before = (row_idx[:, None] > row_idx[None, :]).astype(BF16)
-
-    def route(ids):
-        ids = jnp.pad(ids, ((0, spare), (0, 0)), constant_values=-1)
-        hot = [(ids[:, k : k + 1] == expert_cols).astype(BF16) for k in range(2)]
-        earlier = dot(before, hot[0] + hot[1])
-        picks = []
-        turned = []
-        for k in range(2):
-            within = jnp.sum(earlier * hot[k].astype(F32), axis=1).astype(jnp.int32)
-            slots = ids[:, k] * capacity + within
-            picks.append((slots[:, None] == slot_cols).astype(BF16))
-            turned.append((slots[None, :] == slot_cols[:, None]).astype(BF16))
-        return hot, picks, turned, turned[0] + turned[1], picks[0] + picks[1]
-
-    routed = [route(expert_ids[i]) for i in range(layers)]
-
+    spare = -tok_rows % BLOCK
+    ids = jnp.pad(expert_ids, ((0, 0), (0, spare), (0, 0)), constant_values=-1)
     state = jnp.pad(tokens_in.astype(F32), ((0, spare), (0, 0)))
     saved = []
     for layer_idx in range(layers):
-        hot, picks, turned, turned_both, picks_both = routed[layer_idx]
         got = block_forward(
             (
                 state,
                 spread,
-                turned_both,
-                picks[0],
-                picks[1],
-                hot[0],
-                hot[1],
+                ids[layer_idx],
                 b_in[layer_idx],
                 out_bias[layer_idx],
             ),
@@ -1123,7 +1204,6 @@
     attn_grads = [None] * layers
     expert_grads = [None] * layers
     for layer_idx in reversed(range(layers)):
-        hot, picks, turned, turned_both, picks_both = routed[layer_idx]
         (
             state_in,
             after,
@@ -1145,14 +1225,10 @@
                 (
                     grad_state,
                     spread,
+                    ids[layer_idx],
                     gates,
                     picked0,
                     picked1,
-                    turned[0],
-                    turned[1],
-                    picks_both,
-                    hot[0],
-                    hot[1],
                     after,
                     state_in,
                     qkv,
@@ -1164,23 +1240,24 @@
                 (slope, active, rows_in),
             )
         )
-        attn_grads[layer_idx] = scatter_grads(
-            (h_one, grad_att, h_two), (grad_qkv, heads, grad_logits), sums, spread
-        )[:own_rows]
-    grads = jnp.stack(attn_grads)
-    small = grads[:, :, qkv_cols + out_cols :]
+        attn_grads[layer_idx] = (h_one, grad_att, h_two, grad_qkv, heads, grad_logits, sums)
+    grad_w_qkv, rest, grad_b_in, grad_b_out, grad_w_in, grad_w_exp_out = scatter_grads(
+        attn_grads, spread, expert_grads, own_rows
+    )
+    rest = rest[:, :own_rows]
+    small = rest[:, :, out_cols:]
     return (
         mixed,
         grad_state[:tok_rows],
-        grads[:, :, :qkv_cols].reshape(w_qkv.shape),
-        jnp.swapaxes(grads[:, :, qkv_cols : qkv_cols + out_cols], 1, 2),
+        grad_w_qkv,
+        jnp.swapaxes(rest[:, :, :out_cols], 1, 2),
         small[:, :, :experts],
         jnp.swapaxes(small[:, :, experts : experts + 2], 1, 2),
         jnp.swapaxes(small[:, :, experts + 2 : experts + 5], 1, 2),
-        jnp.stack([parts[0][None] for parts in expert_grads]),
-        jnp.stack([parts[2] for parts in expert_grads]),
-        jnp.stack([parts[1][None] for parts in expert_grads]),
-        jnp.stack([parts[3] for parts in expert_grads]),
+        grad_w_in,
+        grad_b_in,
+        grad_w_exp_out,
+        grad_b_out,
     )
 
 

time: 358 us -> 320 us (0.89)
  other arithmetic: 24.6 us -> 1.85 us
  Pallas kernels: 301 us -> 283 us
  local copies, waits for them, and re-layouts: 23.3 us -> 28.7 us
    pallas_call x3 -> x2, Pallas kernels: 93.1 us -> 78 us  [the longest x1 42 us: scatter_grads(): pl.pallas_call(scatter_kernel, out_shape=(shape((2, own_rows, 3, qkv_cols...]
    convert_element_type x17 -> x0, other arithmetic: 10.6 us -> none  [the longest x4 3.14 us: route(): picks.append((slots[:, None] == slot_cols).astype(BF16))]
    another operation x6 -> x0, other arithmetic: 8.04 us -> none  [the longest x1 4.33 us: on_device(): jnp.stack([parts[0][None] for parts in expert_grads])]
    unnamed x73 -> x58, local copies, waits for them, and re-layouts: 10.8 us -> 16.8 us
  transfers between devices with their start and end apart: 5 -> 5, of which waited for: 0 -> 0; matrix products, arithmetic and copies ran while one was open for 9% -> 3% of each run, Pallas kernels for 25% -> 28%
where the time goes in v1:
time: 320 us; the launch traced here: 316 us
  Pallas kernels  283 us (88%)
  local copies, waits for them, and re-layouts  28.7 us (9%)
    pallas_call x2, Pallas kernels, block_backward(): pl.pallas_call(block_backward_kernel, out_shape=(shape((tokens, width), F...  104 us
    pallas_call x2, Pallas kernels, block_forward(): pl.pallas_call(block_forward_kernel, out_shape=(shape((tokens, width), F3...  101 us
    pallas_call x1, Pallas kernels, scatter_grads(): pl.pallas_call(scatter_kernel, out_shape=(shape((2, own_rows, 3, qkv_cols...  42 us
    pallas_call x1, Pallas kernels, gather_weights(): pl.pallas_call(gather_kernel, out_shape=(whole, whole, jax.ShapeDtypeStru...  36 us
    unnamed x58, local copies, waits for them, and re-layouts  16.8 us
  transfers between devices with their start and end apart: 5, of which 0 were waited for; matrix products, arithmetic and copies ran while one was open for 3% of the time, Pallas kernels for 28%

profile of v1, /device:TPU:0, one launch (start us, length us, event | category | flops | bytes accessed | tf_op | source)
XLA Modules:
  0.0 316.3 jit_solution(5149249452089533810)
XLA Ops:
  0.7 0.1 collective-permute-start
  0.7 3.0 slice_bitcast_fusion.1
  3.7 0.3 collective-permute-start.1
  4.1 1.3 slice_bitcast_fusion
  5.4 0.0 copy-start.11
  5.4 0.0 copy-start.13
  5.4 0.0 copy-start.15
  5.4 0.0 copy-start.18
  5.4 0.0 copy-start.3
  5.4 0.2 collective-permute-start.2
  5.7 0.3 collective-permute-start.3
  6.0 0.2 collective-permute-start.4
  6.2 0.9 pad_convert_fusion.1.state.state_in
  7.1 0.9 pad_convert_fusion.grad_state
  8.0 0.1 copy.27
  8.2 0.6 slice_bitcast_fusion.7
  8.8 0.7 fusion.1
  9.5 0.2 copy.24.w_out
  9.8 36.0 %gather_weights.1 = (bf16[2,32,16,1664]{3,2,1,0:T(8,128)(2,1)S(1)}, bf16[2,32,16,1664]{3,2,1,0:T(8,128)(2,1)S(1)}, bf16[1024,768]{1,0:T(8,128)(2,1)S(1)}) custom-call(bf16[2,12,3,384]{3,2,1,0:T(4,128)(2,1)S(1)} %copy.23.w_qkv, bf16[2,384,12]{2,1,0:T(8,128)(2,1)S(1)} %copy.24.w_out, bf16[2,12,32]{2,1,0:T(8,128)(2,1)S(1)} %copy.25.router, ...), custom_call_target="tpu_custom_call" | custom-call | tf_op jit(solution)/shard_map/gather_weights/pallas_call | solution.py:232
  45.8 1.2 copy-done
  47.0 1.7 copy-done.1
  48.8 1.7 copy-done.2
  50.5 0.0 collective-permute-done
  50.5 0.6 slice_bitcast_fusion.9
  51.1 0.0 collective-permute-done.1.other_in
  51.1 0.0 collective-permute-done.2.other_out
  51.1 53.4 %block_forward.2 = (f32[208,768]{1,0:T(8,128)}, bf16[208,768]{1,0:T(8,128)(2,1)}, f32[208,128]{1,0:T(8,128)}, bf16[208,768]{1,0:T(8,128)(2,1)}, bf16[208,768]{1,...) custom-call(f32[208,768]{1,0:T(8,128)} %pad_convert_fusion.1.state.s, ...), custom_call_target="tpu_custom_call" | custom-call | tf_op jit(solution)/shard_map/block_forward/pallas_call | solution.py:833
  104.5 0.0 collective-permute-done.3.other_in
  104.5 0.0 collective-permute-done.4.other_out
  104.5 47.7 %block_forward.3 = (f32[208,768]{1,0:T(8,128)}, bf16[208,768]{1,0:T(8,128)(2,1)}, f32[208,128]{1,0:T(8,128)}, bf16[208,768]{1,0:T(8,128)(2,1)}, bf16[208,768]{1,...) custom-call(f32[208,768]{1,0:T(8,128)} %get-tuple-element.66.state.s, ...), custom_call_target="tpu_custom_call" | custom-call | tf_op jit(solution)/shard_map/block_forward/pallas_call | solution.py:833
  152.3 51.1 %block_backward.2 = (f32[208,768]{1,0:T(8,128)}, bf16[208,768]{1,0:T(8,128)(2,1)}, bf16[208,128]{1,0:T(8,128)(2,1)}, f32[128,768]{1,0:T(8,128)}, bf16[208,1152]{...) custom-call(f32[208,768]{1,0:T(8,128)} %pad_convert_fusion.grad_state, ...), custom_call_target="tpu_custom_call" | custom-call | tf_op jit(solution)/shard_map/block_backward/pallas_call | solution.py:1102
  203.4 53.2 %block_backward.3 = (f32[208,768]{1,0:T(8,128)}, bf16[208,768]{1,0:T(8,128)(2,1)}, bf16[208,128]{1,0:T(8,128)(2,1)}, f32[128,768]{1,0:T(8,128)}, bf16[208,1152]{...) custom-call(f32[208,768]{1,0:T(8,128)} %get-tuple-element.79.grad_state, ...), custom_call_target="tpu_custom_call" | custom-call | tf_op jit(solution)/shard_map/block_backward/pallas_call | solution.py:1102
  256.6 42.0 %scatter_grads.1 = (f32[2,12,3,384]{3,2,1,0:T(4,128)}, f32[2,16,512]{2,1,0:T(8,128)}, f32[2,1,1536]{2,1,0:T(1,128)}, f32[2,1,384]{2,1,0:T(1,128)}, f32[2,1,384,1...) custom-call(bf16[208,768]{1,0:T(8,128)(2,1)} %get-tuple-element.91.refs_0_, bf16[208,768]{1,0:T(8,128)(2,1)} %get-tuple-element.92.refs_1_, ...), custom_call_target="tpu_custom_call" | custom-call | tf_op jit(solution)/shard_map/scatter_grads/pallas_call | solution.py:444
  298.6 0.8 slice_bitcast_fusion.4
  299.5 0.7 slice.71
  300.2 0.8 slice_bitcast_fusion.6
  301.0 0.8 slice_bitcast_fusion.5
  301.8 1.8 slice.95
  303.6 0.9 slice.69
  304.5 0.7 copy.28
  305.2 0.6 copy.29
  305.8 0.6 copy.30
  306.4 0.7 copy.31
  307.1 0.7 copy.32
  307.7 5.0 %copy.37 = f32[2,1,384,1536]{3,2,1,0:T(8,128)} copy(f32[2,1,384,1536]{3,2,1,0:T(8,128)} %get-tuple-element.158) | data formatting | bytes 9437184
  312.7 0.6 copy.38
  313.4 2.2 copy.39
  315.5 0.6 copy.40
  (42 shorter events, 0.1 us)
Async XLA Ops:
  0.6 3.4 %copy-start.6 = (bf16[2,1,1536,384]{3,2,1,0:T(8,128)(2,1)S(1)}, bf16[2,1,1536,384]{3,2,1,0:T(8,128)(2,1)}, u32[]{:S(2)}) copy-start(bf16[2,1,1536,384]{3,2,1,0:T(8,128)(2,1)} %param.21) | copy-start | bytes 7077892
  0.7 49.9 %collective-permute-start = (bf16[2,1,384]{2,0,1:T(2,128)(2,1)}, bf16[2,1,384]{2,0,1:T(2,128)(2,1)S(1)}, u32[]{:S(2)}, u32[]{:S(2)}) collective-permute-start(bf16[2,1,384]{2,0,1:T(2,128)(2,1)} %param.22), channel_id=1, source_target_pairs={{0,64},{64,0},{1,65},{65,1},{2,66},{66,2},{3,67},{67,3},{4,68},{68... | collective-permute-start | bytes 4616 | tf_op jit(solution)/shard_map/ppermute | solution.py:35
  3.7 1.6 copy-start.4
  3.7 2.5 copy-start.8
  3.7 3.4 %copy-start.9 = (bf16[197,768]{1,0:T(8,128)(2,1)S(1)}, bf16[197,768]{1,0:T(8,128)(2,1)}, u32[]{:S(2)}) copy-start(bf16[197,768]{1,0:T(8,128)(2,1)} %param.23) | copy-start | bytes 907780
  3.7 47.4 %collective-permute-start.1 = (bf16[384,1536]{1,0:T(8,128)(2,1)S(1)}, bf16[384,1536]{1,0:T(8,128)(2,1)}, u32[]{:S(2)}, u32[]{:S(2)}) collective-permute-start(bf16[384,1536]{1,0:T(8,128)(2,1)S(1)} %get-tuple-element.131.own_in), channel_id=1, source_target_pairs={{0,64},{64,0},{1,65},{65,1},{2,66},{66,2},{3,67},{67,3},{4,68},{68... | collective-permute-start | bytes 3538952 | tf_op jit(solution)/shard_map/ppermute | solution.py:35
  5.3 40.5 %copy-start.5 = (bf16[1536,384]{1,0:T(8,128)(2,1)}, bf16[1536,384]{1,0:T(8,128)(2,1)S(1)}, u32[]{:S(2)}) copy-start(bf16[1536,384]{1,0:T(8,128)(2,1)S(1)} %get-tuple-element.129.own_out) | copy-start | bytes 3538948
  5.3 2.7 copy-start.16
  5.3 2.8 copy-start.12
  5.4 4.1 %copy-start.11 = (bf16[2,12,3,384]{3,0,2,1:T(2,128)(2,1)S(1)}, bf16[2,12,3,384]{3,0,2,1:T(2,128)(2,1)}, u32[]{:S(2)}) copy-start(bf16[2,12,3,384]{3,0,2,1:T(2,128)(2,1)} %param.14) | copy-start | bytes 165892
  5.4 4.1 %copy-start.13 = (bf16[2,384,12]{1,0,2:T(2,128)(2,1)S(1)}, bf16[2,384,12]{1,0,2:T(2,128)(2,1)}, u32[]{:S(2)}) copy-start(bf16[2,384,12]{1,0,2:T(2,128)(2,1)} %param.15) | copy-start | bytes 55300
  5.4 4.3 %copy-start.15 = (bf16[2,12,32]{2,0,1:T(2,128)(2,1)S(1)}, bf16[2,12,32]{2,0,1:T(2,128)(2,1)}, u32[]{:S(2)}) copy-start(bf16[2,12,32]{2,0,1:T(2,128)(2,1)} %param.16) | copy-start | bytes 4612
  5.4 4.3 %copy-start.18 = (bf16[2,3,12]{2,0,1:T(2,128)(2,1)S(1)}, bf16[2,3,12]{2,0,1:T(2,128)(2,1)}, u32[]{:S(2)}) copy-start(bf16[2,3,12]{2,0,1:T(2,128)(2,1)} %param.18) | copy-start | bytes 436
  5.4 4.4 %copy-start.3 = (bf16[2,2,12]{2,1,0:T(2,128)(2,1)S(1)}, bf16[2,2,12]{2,1,0:T(2,128)(2,1)}, u32[]{:S(2)}) copy-start(bf16[2,2,12]{2,1,0:T(2,128)(2,1)} %gains.1) | copy-start | bytes 292
  5.4 45.7 %collective-permute-start.2 = (bf16[1536,384]{1,0:T(8,128)(2,1)S(1)}, bf16[1536,384]{1,0:T(8,128)(2,1)}, u32[]{:S(2)}, u32[]{:S(2)}) collective-permute-start(bf16[1536,384]{1,0:T(8,128)(2,1)S(1)} %get-tuple-element.129.own_out), channel_id=1, source_target_pairs={{0,64},{64,0},{1,65},{65,1},{2,66},{66,2},{3,67},{67,3},{4,68},{68... | collective-permute-start | bytes 3538952 | tf_op jit(solution)/shard_map/ppermute | solution.py:35
  5.7 98.9 %collective-permute-start.3 = (bf16[384,1536]{1,0:T(8,128)(2,1)}, bf16[384,1536]{1,0:T(8,128)(2,1)}, u32[]{:S(2)}, u32[]{:S(2)}) collective-permute-start(bf16[384,1536]{1,0:T(8,128)(2,1)} %get-tuple-element.130.own_in), channel_id=1, source_target_pairs={{0,64},{64,0},{1,65},{65,1},{2,66},{66,2},{3,67},{67,3},{4,68},{68... | collective-permute-start | bytes 3538952 | tf_op jit(solution)/shard_map/ppermute | solution.py:35
  6.0 44.5 %copy-start.19 = (bf16[2,1,384]{2,0,1:T(2,128)(2,1)S(1)}, bf16[2,1,384]{2,0,1:T(2,128)(2,1)}, u32[]{:S(2)}) copy-start(bf16[2,1,384]{2,0,1:T(2,128)(2,1)} %param.22) | copy-start | bytes 4612
  6.0 98.5 %collective-permute-start.4 = (bf16[1536,384]{1,0:T(8,128)(2,1)}, bf16[1536,384]{1,0:T(8,128)(2,1)}, u32[]{:S(2)}, u32[]{:S(2)}) collective-permute-start(bf16[1536,384]{1,0:T(8,128)(2,1)} %get-tuple-element.128.own_out), channel_id=1, source_target_pairs={{0,64},{64,0},{1,65},{65,1},{2,66},{66,2},{3,67},{67,3},{4,68},{68... | collective-permute-start | bytes 3538952 | tf_op jit(solution)/shard_map/ppermute | solution.py:35
  45.8 1.2 copy-start
  47.0 1.7 copy-start.1
  48.8 1.7 copy-start.2
  256.6 47.0 %copy-start.7 = (f32[208,768]{1,0:T(8,128)S(1)}, f32[208,768]{1,0:T(8,128)}, u32[]{:S(2)}) copy-start(f32[208,768]{1,0:T(8,128)} %get-tuple-element.90) | copy-start | bytes 1916932
  298.6 5.8 %copy-start.10 = (f32[2,12,3,384]{3,2,1,0:T(4,128)S(1)}, f32[2,12,3,384]{3,2,1,0:T(4,128)}, u32[]{:S(2)}) copy-start(f32[2,12,3,384]{3,2,1,0:T(4,128)} %get-tuple-element.119) | copy-start | bytes 331780
  305.2 8.2 %slice-start = ((s8[4718592]{0:T(1024)(128)(4,1)}), s8[524288]{0:T(1024)(128)(4,1)S(1)}, s32[]{:S(2)}) async-start(s8[4718592]{0:T(1024)(128)(4,1)} %bitcast.32), calls=%async_computation | async-start | bytes 1048576
  307.7 5.0 %copy-start.14 = (f32[2,1,1536]{2,1,0:T(1,128)S(1)}, f32[2,1,1536]{2,1,0:T(1,128)}, u32[]{:S(2)}) copy-start(f32[2,1,1536]{2,1,0:T(1,128)} %get-tuple-element.159) | copy-start | bytes 36868
  307.7 5.6 %slice-start.1 = ((s8[4718592]{0:T(1024)(128)(4,1)}), s8[4194304]{0:T(1024)(128)(4,1)S(1)}, s32[]{:S(2)}) async-start(s8[4718592]{0:T(1024)(128)(4,1)} %bitcast.32), calls=%async_computation.1 | async-start | bytes 8388608
  313.4 2.2 copy-start.17

commit v2 on v1

--- a/solution.py
+++ b/solution.py
@@ -87,7 +87,7 @@
     gains,
     shifts,
     whole0,
-    whole1,
+    later,
     spread,
     mine,
     filled,
@@ -101,7 +101,7 @@
     core_recv,
 ):
     rep, exp, near, far, chip_of = chip_place()
-    wholes = (whole0, whole1)
+    wholes = (whole0,)
 
     def near_copy(layer, step, slot):
         return pltpu.make_async_remote_copy(
@@ -135,7 +135,7 @@
 
     keeps = [
         pltpu.make_async_copy(mine.at[layer], wholes[layer].at[rep, exp], own_sem.at[layer])
-        for layer in range(2)
+        for layer in range(1)
     ]
     barrier = greet(near, far, chip_of, rep)
     layers, own_rows, parts, part_cols = w_qkv.shape
@@ -159,11 +159,14 @@
         vectors[experts + 2 : experts + 5, :] = shifts[layer].astype(F32)
         filled[:, cut:] = dot_nt(turn, vectors[...].astype(BF16))
         filled[:own_rows, cut : cut + experts] = router[layer].astype(F32)
-        mine[layer] = filled[...].astype(BF16)
+        if layer == 0:
+            mine[layer] = filled[...].astype(BF16)
+        else:
+            later[...] = filled[...].astype(BF16)
     for keep in keeps:
         keep.start()
     pl.semaphore_wait(barrier, GREETED)
-    for layer in range(2):
+    for layer in range(1):
 
         @pl.loop(1, NEAR)
         def _(step):
@@ -176,7 +179,7 @@
     spread[...] = jnp.where((inside < own_rows) & (true_row == col), 1.0, 0.0).astype(BF16)
     for keep in keeps:
         keep.wait()
-    for layer in range(2):
+    for layer in range(1):
 
         @pl.loop(0, NEAR)
         def _(back):
@@ -193,7 +196,7 @@
 
             core_copy(layer, source, rep).start()
 
-    for layer in range(2):
+    for layer in range(1):
 
         @pl.loop(0, NEAR)
         def _(back):
@@ -206,7 +209,7 @@
                 far_copy(layer, step, source, slot, slot_far).wait_recv()
                 core_copy(layer, source, rep).start()
 
-    for layer in range(2):
+    for layer in range(1):
 
         @pl.loop(0, NEAR * FAR)
         def _(source):
@@ -233,37 +236,38 @@
         gather_kernel,
         out_shape=(
             whole,
-            whole,
+            jax.ShapeDtypeStruct((BLOCK, cols), BF16),
             jax.ShapeDtypeStruct((devices * BLOCK, devices * own_rows), BF16),
         ),
         in_specs=[VMEM_SPEC] * 5,
-        out_specs=(ANY_SPEC, ANY_SPEC, VMEM_SPEC),
+        out_specs=(ANY_SPEC, VMEM_SPEC, VMEM_SPEC),
         scratch_shapes=[
-            pltpu.VMEM((layers, BLOCK, cols), BF16),
+            pltpu.VMEM((1, BLOCK, cols), BF16),
             pltpu.VMEM((BLOCK, cols), F32),
             pltpu.VMEM((SMALL, own_rows), F32),
-            pltpu.SemaphoreType.DMA((2,)),
-            pltpu.SemaphoreType.DMA((2, NEAR)),
-            pltpu.SemaphoreType.DMA((2, NEAR)),
-            pltpu.SemaphoreType.DMA((2, FAR, NEAR)),
-            pltpu.SemaphoreType.DMA((2, FAR, NEAR)),
-            pltpu.SemaphoreType.DMA((2, NEAR * FAR)),
-            pltpu.SemaphoreType.DMA((2, NEAR * FAR)),
+            pltpu.SemaphoreType.DMA((1,)),
+            pltpu.SemaphoreType.DMA((1, NEAR)),
+            pltpu.SemaphoreType.DMA((1, NEAR)),
+            pltpu.SemaphoreType.DMA((1, FAR, NEAR)),
+            pltpu.SemaphoreType.DMA((1, FAR, NEAR)),
+            pltpu.SemaphoreType.DMA((1, NEAR * FAR)),
+            pltpu.SemaphoreType.DMA((1, NEAR * FAR)),
         ],
         compiler_params=pltpu.CompilerParams(
-            collective_id=0, has_side_effects=True, vmem_limit_bytes=32 << 20
+            collective_id=0, has_side_effects=True, vmem_limit_bytes=60 << 20
         ),
         name="gather_weights",
     )(w_qkv, w_out, router, gains, shifts)
-    return [value.reshape(devices * BLOCK, cols) for value in got[:2]], got[2]
+    return got[0].reshape(devices * BLOCK, cols), got[1], got[2]
 
 
 def scatter_kernel(*refs):
-    per_layer = [refs[7 * layer : 7 * layer + 7] for layer in range(2)]
-    spread = refs[14]
-    biases = refs[15:19]
-    experts = refs[19:23]
-    out_qkv, out_rest, out_b_in, out_b_out, out_in, out_exp = refs[23:29]
+    per_layer = [refs[:7]]
+    done = refs[7]
+    spread = refs[8]
+    biases = refs[9:13]
+    experts = refs[13:17]
+    out_qkv, out_rest, out_b_in, out_b_out, out_in, out_exp = refs[17:23]
     (
         lhs_qkv,
         lhs_proj,
@@ -283,7 +287,7 @@
         far_recv,
         near_send,
         near_recv,
-    ) = refs[29:]
+    ) = refs[23:]
     rep, exp, near, far, chip_of = chip_place()
     qkv_cols, proj_cols = per_layer[0][3].shape[1], per_layer[0][4].shape[1]
     cut = qkv_cols + proj_cols
@@ -344,7 +348,7 @@
         )
 
     barrier = greet(near, far, chip_of, rep)
-    for layer in range(2):
+    for layer in range(1):
         h_one, grad_att, h_two = per_layer[layer][:3]
         lhs_qkv[...] = dot_nt(spread[...], h_one[...]).astype(BF16)
         lhs_proj[...] = dot_nt(spread[...], grad_att[...]).astype(BF16)
@@ -362,7 +366,7 @@
         def _(chunk):
             multiply(layer, rep, chunk)
 
-    for layer in range(2):
+    for layer in range(1):
 
         @pl.loop(0, chunks)
         def _(chunk):
@@ -394,7 +398,7 @@
             value = value + from_far[layer, step, block(slot), :].astype(F32)
         return value
 
-    for layer in range(2):
+    for layer in range(1):
 
         @pl.loop(1, NEAR)
         def _(step):
@@ -405,15 +409,18 @@
     own_rows = out_qkv.shape[1]
     part_cols = qkv_cols // 3
     for layer in range(2):
-        value = add_far(layer, near)
-        for step in range(1, NEAR):
-            near_copy(layer, step).wait_recv()
-            value = value + from_near[layer, step].astype(F32)
+        if layer == 0:
+            value = add_far(layer, near)
+            for step in range(1, NEAR):
+                near_copy(layer, step).wait_recv()
+                value = value + from_near[layer, step].astype(F32)
+        else:
+            value = done[...]
         for idx in range(3):
             out_qkv[layer, :, idx, :] = value[:own_rows, idx * part_cols : (idx + 1) * part_cols]
         out_rest[layer] = value[:, qkv_cols:]
 
-    for layer in range(2):
+    for layer in range(1):
 
         @pl.loop(1, NEAR)
         def _(step):
@@ -433,9 +440,9 @@
         store.wait()
 
 
-def scatter_grads(attn, spread, experts, own_rows):
-    tokens = attn[0][0].shape[0]
-    qkv_cols, proj_cols = attn[0][3].shape[1], attn[0][4].shape[1]
+def scatter_grads(attn, done, spread, experts, own_rows):
+    tokens = attn[0].shape[0]
+    qkv_cols, proj_cols = attn[3].shape[1], attn[4].shape[1]
     cols = qkv_cols + proj_cols + SMALL
     half = NEAR * FAR * BLOCK
     grad_in, grad_exp, grad_b_in, grad_b_out = experts[0]
@@ -451,18 +458,18 @@
             shape((2, 1) + grad_in.shape, F32),
             shape((2, 1) + grad_exp.shape, F32),
         ),
-        in_specs=[VMEM_SPEC] * 19 + [ANY_SPEC] * 4,
+        in_specs=[VMEM_SPEC] * 13 + [ANY_SPEC] * 4,
         out_specs=tuple([VMEM_SPEC] * 4 + [ANY_SPEC] * 2),
         scratch_shapes=[
             pltpu.VMEM((2 * half, tokens), BF16),
             pltpu.VMEM((2 * half, tokens), BF16),
             pltpu.VMEM((2 * half, tokens), BF16),
             pltpu.VMEM((2 * half, SMALL), F32),
-            pltpu.VMEM((2, 2, half, cols), BF16),
-            pltpu.VMEM((2, half, cols), BF16),
-            pltpu.VMEM((2, FAR, NEAR * BLOCK, cols), BF16),
-            pltpu.VMEM((2, NEAR * BLOCK, cols), BF16),
-            pltpu.VMEM((2, NEAR, BLOCK, cols), BF16),
+            pltpu.VMEM((1, 2, half, cols), BF16),
+            pltpu.VMEM((1, half, cols), BF16),
+            pltpu.VMEM((1, FAR, NEAR * BLOCK, cols), BF16),
+            pltpu.VMEM((1, NEAR * BLOCK, cols), BF16),
+            pltpu.VMEM((1, NEAR, BLOCK, cols), BF16),
             pltpu.VMEM((2,) + grad_in.shape, F32),
             pltpu.VMEM((2,) + grad_exp.shape, F32),
             pltpu.SemaphoreType.DMA((4,)),
@@ -474,12 +481,12 @@
             pltpu.SemaphoreType.DMA((2, NEAR)),
         ],
         compiler_params=pltpu.CompilerParams(
-            collective_id=1, has_side_effects=True, vmem_limit_bytes=56 << 20
+            collective_id=1, has_side_effects=True, vmem_limit_bytes=60 << 20
         ),
         name="scatter_grads",
     )(
-        *attn[0],
-        *attn[1],
+        *attn,
+        done,
         spread,
         *(value for parts in experts for value in parts[2:]),
         *(value for parts in experts for value in parts[:2]),
@@ -736,6 +743,7 @@
     recv_sem,
     back_send,
     back_recv,
+    extra=None,
 ):
     exp = lax.axis_index("exp")
     sems = (send_sem, recv_sem, back_send, back_recv)
@@ -749,6 +757,8 @@
     for load in loads:
         load.start()
     barrier = greet_all(exp)
+    if extra:
+        extra.greet(barrier)
     qkv_cols = qkv_out.shape[1]
     cut = qkv_cols + heads_out.shape[1]
     loads[0].wait()
@@ -761,12 +771,16 @@
     h_one_out[...] = h_one
     wide = dot_nt(h_one, spread[...]).astype(BF16)
     qkv_out[...] = dot(wide, whole[:, :qkv_cols]).astype(BF16)
+    if extra:
+        pl.semaphore_wait(barrier, PLANES * PLANE + 1)
+        extra.send()
     attend_forward(qkv_out, heads_out, log_out)
     route(ids, hot0, hot1, pick0, pick1)
     own_att[...] = dot(
         dot_nt(heads_out[...], whole[:, qkv_cols:cut]).astype(BF16), spread[...]
     ).astype(BF16)
-    pl.semaphore_wait(barrier, PLANES * PLANE)
+    if not extra:
+        pl.semaphore_wait(barrier, PLANES * PLANE)
     first = half_copy(own_att, low_att, half_sems, 0)
     first.start()
     first.wait_recv()
@@ -814,6 +828,8 @@
     second.start()
     picked0_out[...] = picked[0].astype(BF16)
     picked1_out[...] = picked[1].astype(BF16)
+    if extra:
+        extra.forward()
     wait_sent(send, rows, back_src, back, exp, sems)
     second.wait_recv()
     next_out[...] = after_out[...] + (own_moe[...].astype(F32) + low_moe[...].astype(F32))
@@ -821,9 +837,66 @@
     second.wait_send()
     for save in saves:
         save.wait()
-
-
-def block_forward(near, whole, weights):
+    if extra:
+        extra.finish()
+
+
+class SpreadRows:
+    def __init__(self, mine, whole, own_sem, send_sem, recv_sem, core_sems):
+        self.rep, self.exp = lax.axis_index("rep"), lax.axis_index("exp")
+        self.mine, self.whole = mine, whole
+        self.send_sem, self.recv_sem = send_sem, recv_sem
+        self.keep = pltpu.make_async_copy(mine, whole.at[self.rep, self.exp], own_sem)
+        self.core = core_send_copy(whole.at[self.rep], whole.at[self.rep], core_sems, 0)
+
+    def copy(self, peer, source):
+        return pltpu.make_async_remote_copy(
+            src_ref=self.mine,
+            dst_ref=self.whole.at[self.rep, self.exp],
+            send_sem=self.send_sem.at[peer],
+            recv_sem=self.recv_sem.at[source],
+            device_id={"exp": peer},
+            device_id_type=MESH,
+        )
+
+    def greet(self, barrier):
+        pl.semaphore_signal(
+            barrier, inc=1, device_id={"rep": 1 - self.rep}, device_id_type=MESH
+        )
+
+    def send(self):
+        self.keep.start()
+
+        @pl.loop(1, PLANES * PLANE)
+        def _(step):
+            self.copy((self.exp + step) % (PLANES * PLANE), self.exp).start()
+
+    def forward(self):
+        @pl.loop(1, PLANES * PLANE)
+        def _(step):
+            source = (self.exp + step) % (PLANES * PLANE)
+            self.copy(source, source).wait_recv()
+
+        self.keep.wait()
+        self.core.start()
+
+    def finish(self):
+        self.core.wait()
+
+        @pl.loop(1, PLANES * PLANE)
+        def _(step):
+            peer = (self.exp + step) % (PLANES * PLANE)
+            self.copy(peer, peer).wait_send()
+
+
+def first_forward_kernel(*refs):
+    inputs, outputs, scratch = refs[:11], refs[11:25], refs[25:]
+    extra = SpreadRows(inputs[10], outputs[13], *scratch[-4:])
+    block_forward_kernel(*inputs[:10], *outputs[:13], *scratch[:-4], extra=extra)
+
+
+def block_forward(near, whole, weights, mine=None):
+    more = mine is not None
     tokens, width = near[0].shape
     slots = BLOCK * PLANES * PLANE
     hidden = weights[0].shape[1]
@@ -831,7 +904,7 @@
     proj = (cols - SMALL) // 4
     shape = jax.ShapeDtypeStruct
     return pl.pallas_call(
-        block_forward_kernel,
+        first_forward_kernel if more else block_forward_kernel,
         out_shape=(
             shape((tokens, width), F32),
             shape((tokens, width), BF16),
@@ -846,9 +919,10 @@
             shape((slots, width), BF16),
             shape((slots, hidden), BF16),
             shape((slots, hidden), BF16),
-        ),
-        in_specs=[VMEM_SPEC] * 5 + [ANY_SPEC] * 5,
-        out_specs=tuple([VMEM_SPEC] * 10 + [ANY_SPEC] * 3),
+        )
+        + ((shape((2, PLANES * PLANE, BLOCK, cols), BF16),) if more else ()),
+        in_specs=[VMEM_SPEC] * 5 + [ANY_SPEC] * (6 if more else 5),
+        out_specs=tuple([VMEM_SPEC] * 10 + [ANY_SPEC] * (4 if more else 3)),
         scratch_shapes=[
             pltpu.VMEM((tokens, 128), BF16),
             pltpu.VMEM((tokens, 128), BF16),
@@ -870,12 +944,17 @@
             pltpu.SemaphoreType.DMA((3,)),
             pltpu.SemaphoreType.DMA((2, 2)),
         ]
-        + row_sems(),
+        + row_sems()
+        + (
+            [pltpu.SemaphoreType.DMA(())] + row_sems()[:2] + [pltpu.SemaphoreType.DMA((1, 2))]
+            if more
+            else []
+        ),
         compiler_params=pltpu.CompilerParams(
-            collective_id=2, has_side_effects=True, vmem_limit_bytes=56 << 20
+            collective_id=4 if more else 2, has_side_effects=True, vmem_limit_bytes=60 << 20
         ),
-        name="block_forward",
-    )(*near, whole, *weights)
+        name="first_forward" if more else "block_forward",
+    )(*near, whole, *weights, *([mine] if more else []))
 
 
 def norm_parts(values):
@@ -960,6 +1039,7 @@
     recv_sem,
     back_send,
     back_recv,
+    extra=None,
 ):
     exp = lax.axis_index("exp")
     rep = lax.axis_index("rep")
@@ -1034,6 +1114,8 @@
     bias_copy.start()
     grad_in_out[...] = dot_tn(kept_rows[:, own_at], inner[...])
 
+    if extra:
+        extra.multiply(spread)
     first.wait_recv()
     total = own_gate[...] + low_gate[...]
     grad0, grad1 = total[:, 0:1], total[:, 1:2]
@@ -1059,6 +1141,8 @@
     grad_b_out_out[...] = bias_own[
         0:1, pl.ds(pl.multiple_of(hidden + rep * half, 128), half)
     ]
+    if extra:
+        extra.send()
     wait_sent(send, rows, back_src, back, exp, sems)
     second.wait_recv()
     grad_h = own_h[...].astype(F32) + low_h[...].astype(F32) + from_router
@@ -1089,9 +1173,111 @@
     put(2, grad_one)
     for copy in (first, second, third, in_copy, exp_copy):
         copy.wait_send()
-
-
-def block_backward(near, whole, weights, kept):
+    if extra:
+        extra.finish()
+
+
+class SumRows:
+    def __init__(
+        self,
+        inputs,
+        out,
+        lhs_qkv,
+        lhs_proj,
+        lhs_small,
+        sums,
+        part,
+        from_core,
+        from_all,
+        core_sems,
+        send_sem,
+        recv_sem,
+    ):
+        self.rep, self.exp = lax.axis_index("rep"), lax.axis_index("exp")
+        self.inputs, self.out = inputs, out
+        self.lhs, self.sums = (lhs_qkv, lhs_proj, lhs_small), sums
+        self.part, self.from_core, self.from_all = part, from_core, from_all
+        self.send_sem, self.recv_sem = send_sem, recv_sem
+        self.core = core_send_copy(part.at[1 - self.rep], from_core, core_sems, 0)
+
+    def multiply(self, spread):
+        rhs = self.inputs[3:6]
+        qkv_cols, cut = rhs[0].shape[1], rhs[0].shape[1] + rhs[1].shape[1]
+        for lhs, rows in zip(self.lhs, self.inputs[:3]):
+            lhs[...] = dot_nt(spread[...], rows[...]).astype(BF16)
+        self.sums[...] = dot_nt(spread[...], self.inputs[6][...].astype(BF16))
+        half = self.from_core.shape[0]
+        rows = BLOCK * 8
+        chunks = half // rows
+        for core in (1 - self.rep, self.rep):
+
+            @pl.loop(0, chunks)
+            def _(chunk):
+                at = pl.ds(pl.multiple_of(core * half + chunk * rows, rows), rows)
+                to = pl.ds(pl.multiple_of(chunk * rows, rows), rows)
+                products = [dot(lhs[at, :], value[...]) for lhs, value in zip(self.lhs, rhs)]
+                self.part[core, to, :qkv_cols] = products[0].astype(BF16)
+                self.part[core, to, qkv_cols:cut] = products[1].astype(BF16)
+                self.part[core, to, cut:] = (products[2] + self.sums[at, :]).astype(BF16)
+
+            if core is not self.rep:
+                self.core.start()
+
+    def copy(self, peer, source):
+        return pltpu.make_async_remote_copy(
+            src_ref=self.part.at[self.rep, block(peer)],
+            dst_ref=self.from_all.at[block(self.exp)],
+            send_sem=self.send_sem.at[peer],
+            recv_sem=self.recv_sem.at[source],
+            device_id={"exp": peer},
+            device_id_type=MESH,
+        )
+
+    def send(self):
+        self.core.wait_recv()
+        rows = BLOCK * 8
+
+        @pl.loop(0, self.from_core.shape[0] // rows)
+        def _(chunk):
+            to = pl.ds(pl.multiple_of(chunk * rows, rows), rows)
+            self.part[self.rep, to, :] = (
+                self.part[self.rep, to, :].astype(F32) + self.from_core[to, :].astype(F32)
+            ).astype(BF16)
+
+        @pl.loop(1, PLANES * PLANE)
+        def _(step):
+            self.copy((self.exp + step) % (PLANES * PLANE), self.exp).start()
+
+    def finish(self):
+        self.from_all[block(self.exp), :] = self.part[self.rep, block(self.exp), :]
+
+        @pl.loop(1, PLANES * PLANE)
+        def _(step):
+            source = (self.exp + step) % (PLANES * PLANE)
+            self.copy(source, source).wait_recv()
+
+        self.out[...] = jnp.zeros_like(self.out)
+
+        @pl.loop(0, PLANES * PLANE)
+        def _(source):
+            self.out[...] += self.from_all[block(source), :].astype(F32)
+
+        @pl.loop(1, PLANES * PLANE)
+        def _(step):
+            peer = (self.exp + step) % (PLANES * PLANE)
+            self.copy(peer, peer).wait_send()
+
+        self.core.wait_send()
+
+
+def last_backward_kernel(*refs):
+    inputs, outputs, scratch = refs[:26], refs[26:36], refs[36:]
+    extra = SumRows(inputs[19:], outputs[9], *scratch[-10:])
+    block_backward_kernel(*inputs[:19], *outputs[:9], *scratch[:-10], extra=extra)
+
+
+def block_backward(near, whole, weights, kept, later=()):
+    more = len(later) > 0
     tokens, width = near[0].shape
     slots = BLOCK * PLANES * PLANE
     hidden = weights[0].shape[1]
@@ -1100,7 +1286,7 @@
     half = width // 2
     shape = jax.ShapeDtypeStruct
     return pl.pallas_call(
-        block_backward_kernel,
+        last_backward_kernel if more else block_backward_kernel,
         out_shape=(
             shape((tokens, width), F32),
             shape((tokens, width), BF16),
@@ -1111,9 +1297,10 @@
             shape((hidden, half), F32),
             shape((1, hidden), F32),
             shape((1, half), F32),
-        ),
-        in_specs=[VMEM_SPEC] * 11 + [ANY_SPEC] * 8,
-        out_specs=tuple([VMEM_SPEC] * 9),
+        )
+        + ((shape((BLOCK, cols), F32),) if more else ()),
+        in_specs=[VMEM_SPEC] * 11 + [ANY_SPEC] * 8 + [VMEM_SPEC] * len(later),
+        out_specs=tuple([VMEM_SPEC] * (10 if more else 9)),
         scratch_shapes=[
             pltpu.VMEM((tokens, 128), BF16),
             pltpu.VMEM((tokens, 128), BF16),
@@ -1147,12 +1334,25 @@
             pltpu.SemaphoreType.DMA((3, 2)),
             pltpu.SemaphoreType.DMA((3, 2)),
         ]
-        + row_sems(),
+        + row_sems()
+        + (
+            [pltpu.VMEM((2 * slots, tokens), BF16)] * 3
+            + [
+                pltpu.VMEM((2 * slots, SMALL), F32),
+                pltpu.VMEM((2, slots, cols), BF16),
+                pltpu.VMEM((slots, cols), BF16),
+                pltpu.VMEM((slots, cols), BF16),
+                pltpu.SemaphoreType.DMA((1, 2)),
+            ]
+            + row_sems()[:2]
+            if more
+            else []
+        ),
         compiler_params=pltpu.CompilerParams(
-            collective_id=3, has_side_effects=True, vmem_limit_bytes=56 << 20
+            collective_id=5 if more else 3, has_side_effects=True, vmem_limit_bytes=60 << 20
         ),
-        name="block_backward",
-    )(*near, whole, *weights, *kept)
+        name="last_backward" if more else "block_backward",
+    )(*near, whole, *weights, *kept, *later)
 
 
 def on_device(
@@ -1174,7 +1374,7 @@
     own_rows = w_qkv.shape[1]
     out_cols = w_out.shape[1]
     experts = w_in.shape[1] * lax.axis_size("exp")
-    wholes, spread = gather_weights(w_qkv, w_out, router, gains, shifts)
+    whole, later_rows, spread = gather_weights(w_qkv, w_out, router, gains, shifts)
     expert_w = []
     for layer_idx in range(layers):
         own_in, own_out = w_in[layer_idx, 0], w_exp_out[layer_idx, 0]
@@ -1194,10 +1394,13 @@
                 b_in[layer_idx],
                 out_bias[layer_idx],
             ),
-            wholes[layer_idx],
+            whole,
             expert_w[layer_idx],
-        )
-        saved.append((state,) + tuple(got))
+            later_rows if layer_idx == 0 else None,
+        )
+        saved.append((state, whole) + tuple(got[:13]))
+        if layer_idx == 0:
+            whole = got[13].reshape(whole.shape)
         state = got[5]
     mixed = state[:tok_rows].astype(BF16)
     grad_state = jnp.pad(cotangent.astype(F32), ((0, spare), (0, 0)))
@@ -1206,6 +1409,7 @@
     for layer_idx in reversed(range(layers)):
         (
             state_in,
+            whole,
             after,
             h_two,
             gates,
@@ -1220,7 +1424,7 @@
             slope,
             active,
         ) = saved[layer_idx]
-        grad_state, grad_att, grad_logits, sums, grad_qkv, *expert_grads[layer_idx] = (
+        grad_state, grad_att, grad_logits, sums, grad_qkv, *rest = (
             block_backward(
                 (
                     grad_state,
@@ -1235,14 +1439,16 @@
                     log_total,
                     heads,
                 ),
-                wholes[layer_idx],
+                whole,
                 expert_w[layer_idx],
                 (slope, active, rows_in),
+                attn_grads[layer_idx + 1] if layer_idx + 1 < layers else (),
             )
         )
+        expert_grads[layer_idx] = rest[:4]
         attn_grads[layer_idx] = (h_one, grad_att, h_two, grad_qkv, heads, grad_logits, sums)
     grad_w_qkv, rest, grad_b_in, grad_b_out, grad_w_in, grad_w_exp_out = scatter_grads(
-        attn_grads, spread, expert_grads, own_rows
+        attn_grads[0], rest[4], spread, expert_grads, own_rows
     )
     rest = rest[:, :own_rows]
     small = rest[:, :, out_cols:]

time: 320 us -> 343 us (1.072)
  Pallas kernels: 283 us -> 303 us
    pallas_call x5, Pallas kernels: 241 us -> 274 us  [the longest x2 123 us: block_forward(): pl.pallas_call(first_forward_kernel if more else block_forward_kernel, ou...]
    pallas_call x1, Pallas kernels: 42 us -> 28.6 us  [scatter_grads(): pl.pallas_call(scatter_kernel, out_shape=(shape((2, own_rows, 3, qkv_cols...]
    unnamed x58 -> x42, local copies, waits for them, and re-layouts: 16.8 us -> 18.1 us
  transfers between devices with their start and end apart: 5 -> 5, of which waited for: 0 -> 0; matrix products, arithmetic and copies ran while one was open for 3% -> 4% of each run, Pallas kernels for 28% -> 30%
where the time goes in v2:
time: 343 us; the launch traced here: 337 us
  Pallas kernels  303 us (88%)
  local copies, waits for them, and re-layouts  30 us (9%)
    pallas_call x2, Pallas kernels, block_forward(): pl.pallas_call(first_forward_kernel if more else block_forward_kernel, ou...  123 us
    pallas_call x2, Pallas kernels, block_backward(): pl.pallas_call(last_backward_kernel if more else block_backward_kernel, o...  123 us
    pallas_call x1, Pallas kernels, scatter_grads(): pl.pallas_call(scatter_kernel, out_shape=(shape((2, own_rows, 3, qkv_cols...  28.6 us
    pallas_call x1, Pallas kernels, gather_weights(): pl.pallas_call(gather_kernel, out_shape=(whole, jax.ShapeDtypeStruct((BLO...  27.5 us
    unnamed x42, local copies, waits for them, and re-layouts  18.1 us
  transfers between devices with their start and end apart: 5, of which 0 were waited for; matrix products, arithmetic and copies ran while one was open for 4% of the time, Pallas kernels for 30%

profile of v2, /device:TPU:0, one launch (start us, length us, event | category | flops | bytes accessed | tf_op | source)
XLA Modules:
  0.0 337.4 jit_solution(814187774761130731)
XLA Ops:
  0.7 0.1 collective-permute-start
  0.7 1.9 slice_bitcast_fusion.1
  2.7 0.0 copy-start
  2.7 0.0 copy-start.5
  2.7 0.0 copy-start.6
  2.7 0.4 collective-permute-start.1
  3.2 1.3 slice_bitcast_fusion
  4.5 0.2 collective-permute-start.2
  4.7 0.4 collective-permute-start.3
  5.1 0.1 collective-permute-start.4
  5.2 0.9 pad_convert_fusion.1.refs_0_.refs_7_
  6.1 0.9 pad_convert_fusion.grad_state
  6.9 1.5 copy.27
  8.4 0.6 slice_bitcast_fusion.7
  9.0 1.6 fusion.1
  10.7 1.5 copy.23.w_qkv
  12.1 1.6 copy.24.w_out
  13.7 0.0 copy-done.10
  13.7 0.6 copy.25.router
  14.3 1.3 copy.26.shifts
  15.6 27.5 %gather_weights.1 = (bf16[2,32,16,1664]{3,2,1,0:T(8,128)(2,1)}, bf16[16,1664]{1,0:T(8,128)(2,1)}, bf16[1024,768]{1,0:T(8,128)(2,1)}) custom-call(bf16[2,12,3,384]{3,2,1,0:T(4,128)(2,1)} %copy.23.w_qkv, bf16[2,384,12]{2,1,0:T(8,128)(2,1)} %copy.24.w_out, bf16[2,12,32]{2,1,0:T(8,128)(2,1)} %copy.25.router, bf16[2,2,12]{2,1,0:T(2,128)(2,1)} %gains.1, ...), custom_call_target="tpu_custom_call" | custom-call | tf_op jit(solution)/shard_map/gather_weights/pallas_call | solution.py:235
  43.1 0.0 collective-permute-done
  43.1 0.7 broadcast_select_fusion.1
  43.8 0.6 slice_bitcast_fusion.9
  44.4 0.0 collective-permute-done.1.refs_7_.refs_13_
  44.4 0.0 collective-permute-done.2.refs_9_.refs_15_
  44.4 73.7 %first_forward.1 = (f32[208,768]{1,0:T(8,128)}, bf16[208,768]{1,0:T(8,128)(2,1)}, f32[208,128]{1,0:T(8,128)}, bf16[208,768]{1,0:T(8,128)(2,1)}, bf16[208,768]{1,...) custom-call(f32[208,768]{1,0:T(8,128)} %pad_convert_fusion.1.refs_0_, ...), custom_call_target="tpu_custom_call" | custom-call | tf_op jit(solution)/shard_map/first_forward/pallas_call | solution.py:906
  118.1 0.0 collective-permute-done.3.other_in
  118.1 0.0 collective-permute-done.4.other_out
  118.1 49.6 %block_forward.1 = (f32[208,768]{1,0:T(8,128)}, bf16[208,768]{1,0:T(8,128)(2,1)}, f32[208,128]{1,0:T(8,128)}, bf16[208,768]{1,0:T(8,128)(2,1)}, bf16[208,768]{1,...) custom-call(f32[208,768]{1,0:T(8,128)} %get-tuple-element.69.state.s, ...), custom_call_target="tpu_custom_call" | custom-call | tf_op jit(solution)/shard_map/block_forward/pallas_call | solution.py:906
  167.7 51.2 %block_backward.1 = (f32[208,768]{1,0:T(8,128)}, bf16[208,768]{1,0:T(8,128)(2,1)}, bf16[208,128]{1,0:T(8,128)(2,1)}, f32[128,768]{1,0:T(8,128)}, bf16[208,1152]{...) custom-call(f32[208,768]{1,0:T(8,128)} %pad_convert_fusion.grad_state, ...), custom_call_target="tpu_custom_call" | custom-call | tf_op jit(solution)/shard_map/block_backward/pallas_call | solution.py:1288
  219.0 72.0 %last_backward.1 = (f32[208,768]{1,0:T(8,128)}, bf16[208,768]{1,0:T(8,128)(2,1)}, bf16[208,128]{1,0:T(8,128)(2,1)}, f32[128,768]{1,0:T(8,128)}, bf16[208,1152]{1...) custom-call(f32[208,768]{1,0:T(8,128)} %get-tuple-element.82.refs_0_, ...), custom_call_target="tpu_custom_call" | custom-call | tf_op jit(solution)/shard_map/last_backward/pallas_call | solution.py:1288
  291.0 28.6 %scatter_grads.1 = (f32[2,12,3,384]{3,2,1,0:T(4,128)}, f32[2,16,512]{2,1,0:T(8,128)}, f32[2,1,1536]{2,1,0:T(1,128)}, f32[2,1,384]{2,1,0:T(1,128)}, f32[2,1,384,1...) custom-call(bf16[208,768]{1,0:T(8,128)(2,1)} %get-tuple-element.100.refs_0_, bf16[208,768]{1,0:T(8,128)(2,1)} %get-tuple-element.101.refs_1_, ...), custom_call_target="tpu_custom_call" | custom-call | tf_op jit(solution)/shard_map/scatter_grads/pallas_call | solution.py:451
  319.7 0.8 slice_bitcast_fusion.4
  320.5 0.7 slice.71
  321.2 0.8 slice_bitcast_fusion.6
  322.0 0.8 slice_bitcast_fusion.5
  322.8 1.8 slice.95
  324.6 0.9 slice.69
  325.5 0.7 copy.28
  326.2 0.6 copy.29
  326.8 0.6 copy.30
  327.4 0.7 copy.31
  328.1 0.7 copy.32
  328.8 5.0 %copy.37 = f32[2,1,384,1536]{3,2,1,0:T(8,128)} copy(f32[2,1,384,1536]{3,2,1,0:T(8,128)} %get-tuple-element.162) | data formatting | bytes 9437184
  333.8 0.6 copy.38
  334.4 2.2 copy.39
  336.6 0.6 copy.40
  (26 shorter events, 0.1 us)
Async XLA Ops:
  0.6 2.5 copy-start.3
  0.7 42.4 %collective-permute-start = (bf16[2,1,384]{2,0,1:T(2,128)(2,1)}, bf16[2,1,384]{2,0,1:T(2,128)(2,1)}, u32[]{:S(2)}, u32[]{:S(2)}) collective-permute-start(bf16[2,1,384]{2,0,1:T(2,128)(2,1)} %param.22), channel_id=1, source_target_pairs={{0,64},{64,0},{1,65},{65,1},{2,66},{66,2},{3,67},{67,3},{4,68},{68... | collective-permute-start | bytes 4616 | tf_op jit(solution)/shard_map/ppermute | solution.py:35
  2.7 1.8 copy-start
  2.7 2.0 copy-start.2
  2.7 2.5 copy-start.5
  2.7 3.3 copy-start.6
  2.7 41.7 %collective-permute-start.1 = (bf16[384,1536]{1,0:T(8,128)(2,1)S(1)}, bf16[384,1536]{1,0:T(8,128)(2,1)}, u32[]{:S(2)}, u32[]{:S(2)}) collective-permute-start(bf16[384,1536]{1,0:T(8,128)(2,1)S(1)} %get-tuple-element.135.refs_6_.refs_12_), channel_id=1, source_target_pairs={{0,64},{64,0},{1,65},{65,1},{2,66},{66,2},{3,67},{67,3},{4,68},{68... | collective-permute-start | bytes 3538952 | tf_op jit(solution)/shard_map/ppermute | solution.py:35
  4.5 38.6 %copy-start.1 = (bf16[1536,384]{1,0:T(8,128)(2,1)}, bf16[1536,384]{1,0:T(8,128)(2,1)S(1)}, u32[]{:S(2)}) copy-start(bf16[1536,384]{1,0:T(8,128)(2,1)S(1)} %get-tuple-element.133.refs_8_.refs_14_) | copy-start | bytes 3538948
  4.5 4.0 %copy-start.8 = (bf16[2,1,1536]{2,0,1:T(2,128)(2,1)S(1)}, bf16[2,1,1536]{2,0,1:T(2,128)(2,1)}, u32[]{:S(2)}) copy-start(bf16[2,1,1536]{2,0,1:T(2,128)(2,1)} %param.20) | copy-start | bytes 18436
  4.5 9.2 %copy-start.10 = (bf16[2,12,32]{2,0,1:T(2,128)(2,1)S(1)}, bf16[2,12,32]{2,0,1:T(2,128)(2,1)}, u32[]{:S(2)}) copy-start(bf16[2,12,32]{2,0,1:T(2,128)(2,1)} %param.16) | copy-start | bytes 4612
  4.5 39.9 %collective-permute-start.2 = (bf16[1536,384]{1,0:T(8,128)(2,1)S(1)}, bf16[1536,384]{1,0:T(8,128)(2,1)}, u32[]{:S(2)}, u32[]{:S(2)}) collective-permute-start(bf16[1536,384]{1,0:T(8,128)(2,1)S(1)} %get-tuple-element.133.refs_8_.refs_14_), channel_id=1, source_target_pairs={{0,64},{64,0},{1,65},{65,1},{2,66},{66,2},{3,67},{67,3},{4,68},{68... | collective-permute-start | bytes 3538952 | tf_op jit(solution)/shard_map/ppermute | solution.py:35
  4.7 113.5 %collective-permute-start.3 = (bf16[384,1536]{1,0:T(8,128)(2,1)S(1)}, bf16[384,1536]{1,0:T(8,128)(2,1)}, u32[]{:S(2)}, u32[]{:S(2)}) collective-permute-start(bf16[384,1536]{1,0:T(8,128)(2,1)S(1)} %get-tuple-element.134.own_in), channel_id=1, source_target_pairs={{0,64},{64,0},{1,65},{65,1},{2,66},{66,2},{3,67},{67,3},{4,68},{68... | collective-permute-start | bytes 3538952 | tf_op jit(solution)/shard_map/ppermute | solution.py:35
  5.1 113.1 %collective-permute-start.4 = (bf16[1536,384]{1,0:T(8,128)(2,1)}, bf16[1536,384]{1,0:T(8,128)(2,1)}, u32[]{:S(2)}, u32[]{:S(2)}) collective-permute-start(bf16[1536,384]{1,0:T(8,128)(2,1)} %get-tuple-element.132.own_out), channel_id=1, source_target_pairs={{0,64},{64,0},{1,65},{65,1},{2,66},{66,2},{3,67},{67,3},{4,68},{68... | collective-permute-start | bytes 3538952 | tf_op jit(solution)/shard_map/ppermute | solution.py:35
  291.0 33.6 %copy-start.4 = (f32[208,768]{1,0:T(8,128)S(1)}, f32[208,768]{1,0:T(8,128)}, u32[]{:S(2)}) copy-start(f32[208,768]{1,0:T(8,128)} %get-tuple-element.99) | copy-start | bytes 1916932
  319.6 5.8 %copy-start.7 = (f32[2,12,3,384]{3,2,1,0:T(4,128)S(1)}, f32[2,12,3,384]{3,2,1,0:T(4,128)}, u32[]{:S(2)}) copy-start(f32[2,12,3,384]{3,2,1,0:T(4,128)} %get-tuple-element.123) | copy-start | bytes 331780
  326.2 8.2 %slice-start = ((s8[4718592]{0:T(1024)(128)(4,1)}), s8[524288]{0:T(1024)(128)(4,1)S(1)}, s32[]{:S(2)}) async-start(s8[4718592]{0:T(1024)(128)(4,1)} %bitcast.32), calls=%async_computation | async-start | bytes 1048576
  328.8 5.0 %copy-start.9 = (f32[2,1,1536]{2,1,0:T(1,128)S(1)}, f32[2,1,1536]{2,1,0:T(1,128)}, u32[]{:S(2)}) copy-start(f32[2,1,1536]{2,1,0:T(1,128)} %get-tuple-element.163) | copy-start | bytes 36868
  328.8 5.6 %slice-start.1 = ((s8[4718592]{0:T(1024)(128)(4,1)}), s8[4194304]{0:T(1024)(128)(4,1)S(1)}, s32[]{:S(2)}) async-start(s8[4718592]{0:T(1024)(128)(4,1)} %bitcast.32), calls=%async_computation.1 | async-start | bytes 8388608
  334.4 2.2 copy-start.11

commit v3 on v1

--- a/solution.py
+++ b/solution.py
@@ -1019,19 +1019,6 @@
     in_away[...] = dot_tn(kept_rows[:, other_at], inner[...]).astype(BF16)
     in_copy = core_send_copy(in_away, in_got, core_sems, 0)
     in_copy.start()
-    tall = product.shape[0]
-    for start in range(0, hidden, tall):
-        part = slice(start, start + tall)
-        product[...] = dot_tn(active[:, part], rows[...])
-        grad_exp_out[part, :] = product[:, own_at]
-        exp_away[part, :] = product[:, other_at].astype(BF16)
-    exp_copy = core_send_copy(exp_away, exp_got, core_sems, 1)
-    exp_copy.start()
-    bias_own[...] = jnp.zeros_like(bias_own)
-    bias_own[0:1, :hidden] = jnp.sum(inner[...].astype(F32), axis=0, keepdims=True)
-    bias_own[0:1, hidden:] = jnp.sum(rows[...].astype(F32), axis=0, keepdims=True)
-    bias_copy = core_send_copy(bias_own, bias_got, core_sems, 2)
-    bias_copy.start()
     grad_in_out[...] = dot_tn(kept_rows[:, own_at], inner[...])
 
     first.wait_recv()
@@ -1049,16 +1036,19 @@
     own_h[...] = dot(pick0[...] + pick1[...], back[...]).astype(BF16)
     second = half_copy(own_h, low_h, half_sems, 1)
     second.start()
-    in_copy.wait_recv()
-    grad_in_out[...] += in_got[...].astype(F32)
-    exp_copy.wait_recv()
-    grad_exp_out[...] += exp_got[...].astype(F32)
-    bias_copy.wait()
-    bias_own[...] += bias_got[...]
-    grad_b_in_out[...] = bias_own[0:1, :hidden]
-    grad_b_out_out[...] = bias_own[
-        0:1, pl.ds(pl.multiple_of(hidden + rep * half, 128), half)
-    ]
+    tall = product.shape[0]
+    for start in range(0, hidden, tall):
+        part = slice(start, start + tall)
+        product[...] = dot_tn(active[:, part], rows[...])
+        grad_exp_out[part, :] = product[:, own_at]
+        exp_away[part, :] = product[:, other_at].astype(BF16)
+    exp_copy = core_send_copy(exp_away, exp_got, core_sems, 1)
+    exp_copy.start()
+    bias_own[...] = jnp.zeros_like(bias_own)
+    bias_own[0:1, :hidden] = jnp.sum(inner[...].astype(F32), axis=0, keepdims=True)
+    bias_own[0:1, hidden:] = jnp.sum(rows[...].astype(F32), axis=0, keepdims=True)
+    bias_copy = core_send_copy(bias_own, bias_got, core_sems, 2)
+    bias_copy.start()
     wait_sent(send, rows, back_src, back, exp, sems)
     second.wait_recv()
     grad_h = own_h[...].astype(F32) + low_h[...].astype(F32) + from_router
@@ -1081,6 +1071,16 @@
     ).astype(BF16)
     third = half_copy(own_one, low_one, half_sems, 2)
     third.start()
+    in_copy.wait_recv()
+    grad_in_out[...] += in_got[...].astype(F32)
+    exp_copy.wait_recv()
+    grad_exp_out[...] += exp_got[...].astype(F32)
+    bias_copy.wait()
+    bias_own[...] += bias_got[...]
+    grad_b_in_out[...] = bias_own[0:1, :hidden]
+    grad_b_out_out[...] = bias_own[
+        0:1, pl.ds(pl.multiple_of(hidden + rep * half, 128), half)
+    ]
     unit, scale = norm_parts(state_in[...])
     third.wait_recv()
     grad_one = own_one[...].astype(F32) + low_one[...].astype(F32)

time: 320 us -> 320 us (level)
  no operation moved by 1% of the time
where the time goes in v3:
time: 320 us; the launch traced here: 317 us
  Pallas kernels  284 us (89%)
  local copies, waits for them, and re-layouts  28.7 us (9%)
    pallas_call x2, Pallas kernels, block_backward(): pl.pallas_call(block_backward_kernel, out_shape=(shape((tokens, width), F...  104 us
    pallas_call x2, Pallas kernels, block_forward(): pl.pallas_call(block_forward_kernel, out_shape=(shape((tokens, width), F3...  101 us
    pallas_call x1, Pallas kernels, scatter_grads(): pl.pallas_call(scatter_kernel, out_shape=(shape((2, own_rows, 3, qkv_cols...  42.1 us
    pallas_call x1, Pallas kernels, gather_weights(): pl.pallas_call(gather_kernel, out_shape=(whole, whole, jax.ShapeDtypeStru...  36 us
    unnamed x58, local copies, waits for them, and re-layouts  16.8 us
  transfers between devices with their start and end apart: 5, of which 0 were waited for; matrix products, arithmetic and copies ran while one was open for 3% of the time, Pallas kernels for 28%

profile of v3, /device:TPU:0, one launch (start us, length us, event | category | flops | bytes accessed | tf_op | source)
XLA Modules:
  0.0 316.6 jit_solution(10446745966634270610)
XLA Ops:
  0.7 0.1 collective-permute-start
  0.7 3.0 slice_bitcast_fusion.1
  3.7 0.3 collective-permute-start.1
  4.1 1.3 slice_bitcast_fusion
  5.4 0.0 copy-start.11
  5.4 0.0 copy-start.13
  5.4 0.0 copy-start.15
  5.4 0.0 copy-start.18
  5.4 0.0 copy-start.3
  5.4 0.2 collective-permute-start.2
  5.7 0.3 collective-permute-start.3
  6.0 0.2 collective-permute-start.4
  6.2 0.9 pad_convert_fusion.1.state.state_in
  7.1 0.9 pad_convert_fusion.grad_state
  8.0 0.1 copy.27
  8.2 0.6 slice_bitcast_fusion.7
  8.8 0.7 fusion.1
  9.5 0.2 copy.24.w_out
  9.8 36.0 %gather_weights.1 = (bf16[2,32,16,1664]{3,2,1,0:T(8,128)(2,1)S(1)}, bf16[2,32,16,1664]{3,2,1,0:T(8,128)(2,1)S(1)}, bf16[1024,768]{1,0:T(8,128)(2,1)S(1)}) custom-call(bf16[2,12,3,384]{3,2,1,0:T(4,128)(2,1)S(1)} %copy.23.w_qkv, bf16[2,384,12]{2,1,0:T(8,128)(2,1)S(1)} %copy.24.w_out, bf16[2,12,32]{2,1,0:T(8,128)(2,1)S(1)} %copy.25.router, ...), custom_call_target="tpu_custom_call" | custom-call | tf_op jit(solution)/shard_map/gather_weights/pallas_call | solution.py:232
  45.8 1.2 copy-done
  47.0 1.7 copy-done.1
  48.8 1.7 copy-done.2
  50.5 0.0 collective-permute-done
  50.5 0.6 slice_bitcast_fusion.9
  51.1 0.0 collective-permute-done.1.other_in
  51.1 0.0 collective-permute-done.2.other_out
  51.1 53.4 %block_forward.2 = (f32[208,768]{1,0:T(8,128)}, bf16[208,768]{1,0:T(8,128)(2,1)}, f32[208,128]{1,0:T(8,128)}, bf16[208,768]{1,0:T(8,128)(2,1)}, bf16[208,768]{1,...) custom-call(f32[208,768]{1,0:T(8,128)} %pad_convert_fusion.1.state.s, ...), custom_call_target="tpu_custom_call" | custom-call | tf_op jit(solution)/shard_map/block_forward/pallas_call | solution.py:833
  104.5 0.0 collective-permute-done.3.other_in
  104.5 0.0 collective-permute-done.4.other_out
  104.5 47.7 %block_forward.3 = (f32[208,768]{1,0:T(8,128)}, bf16[208,768]{1,0:T(8,128)(2,1)}, f32[208,128]{1,0:T(8,128)}, bf16[208,768]{1,0:T(8,128)(2,1)}, bf16[208,768]{1,...) custom-call(f32[208,768]{1,0:T(8,128)} %get-tuple-element.66.state.s, ...), custom_call_target="tpu_custom_call" | custom-call | tf_op jit(solution)/shard_map/block_forward/pallas_call | solution.py:833
  152.3 51.3 %block_backward.2 = (f32[208,768]{1,0:T(8,128)}, bf16[208,768]{1,0:T(8,128)(2,1)}, bf16[208,128]{1,0:T(8,128)(2,1)}, f32[128,768]{1,0:T(8,128)}, bf16[208,1152]{...) custom-call(f32[208,768]{1,0:T(8,128)} %pad_convert_fusion.grad_state, ...), custom_call_target="tpu_custom_call" | custom-call | tf_op jit(solution)/shard_map/block_backward/pallas_call | solution.py:1102
  203.5 53.2 %block_backward.3 = (f32[208,768]{1,0:T(8,128)}, bf16[208,768]{1,0:T(8,128)(2,1)}, bf16[208,128]{1,0:T(8,128)(2,1)}, f32[128,768]{1,0:T(8,128)}, bf16[208,1152]{...) custom-call(f32[208,768]{1,0:T(8,128)} %get-tuple-element.79.grad_state, ...), custom_call_target="tpu_custom_call" | custom-call | tf_op jit(solution)/shard_map/block_backward/pallas_call | solution.py:1102
  256.8 42.1 %scatter_grads.1 = (f32[2,12,3,384]{3,2,1,0:T(4,128)}, f32[2,16,512]{2,1,0:T(8,128)}, f32[2,1,1536]{2,1,0:T(1,128)}, f32[2,1,384]{2,1,0:T(1,128)}, f32[2,1,384,1...) custom-call(bf16[208,768]{1,0:T(8,128)(2,1)} %get-tuple-element.91.refs_0_, bf16[208,768]{1,0:T(8,128)(2,1)} %get-tuple-element.92.refs_1_, ...), custom_call_target="tpu_custom_call" | custom-call | tf_op jit(solution)/shard_map/scatter_grads/pallas_call | solution.py:444
  298.9 0.8 slice_bitcast_fusion.4
  299.7 0.7 slice.71
  300.4 0.8 slice_bitcast_fusion.6
  301.2 0.8 slice_bitcast_fusion.5
  302.0 1.8 slice.95
  303.8 0.9 slice.69
  304.7 0.7 copy.28
  305.4 0.6 copy.29
  306.0 0.6 copy.30
  306.6 0.7 copy.31
  307.3 0.7 copy.32
  308.0 5.0 %copy.37 = f32[2,1,384,1536]{3,2,1,0:T(8,128)} copy(f32[2,1,384,1536]{3,2,1,0:T(8,128)} %get-tuple-element.158) | data formatting | bytes 9437184
  313.0 0.6 copy.38
  313.6 2.2 copy.39
  315.8 0.6 copy.40
  (42 shorter events, 0.1 us)
Async XLA Ops:
  0.6 3.4 %copy-start.6 = (bf16[2,1,1536,384]{3,2,1,0:T(8,128)(2,1)S(1)}, bf16[2,1,1536,384]{3,2,1,0:T(8,128)(2,1)}, u32[]{:S(2)}) copy-start(bf16[2,1,1536,384]{3,2,1,0:T(8,128)(2,1)} %param.21) | copy-start | bytes 7077892
  0.7 49.9 %collective-permute-start = (bf16[2,1,384]{2,0,1:T(2,128)(2,1)}, bf16[2,1,384]{2,0,1:T(2,128)(2,1)S(1)}, u32[]{:S(2)}, u32[]{:S(2)}) collective-permute-start(bf16[2,1,384]{2,0,1:T(2,128)(2,1)} %param.22), channel_id=1, source_target_pairs={{0,64},{64,0},{1,65},{65,1},{2,66},{66,2},{3,67},{67,3},{4,68},{68... | collective-permute-start | bytes 4616 | tf_op jit(solution)/shard_map/ppermute | solution.py:35
  3.7 1.6 copy-start.4
  3.7 2.5 copy-start.8
  3.7 3.4 %copy-start.9 = (bf16[197,768]{1,0:T(8,128)(2,1)S(1)}, bf16[197,768]{1,0:T(8,128)(2,1)}, u32[]{:S(2)}) copy-start(bf16[197,768]{1,0:T(8,128)(2,1)} %param.23) | copy-start | bytes 907780
  3.7 47.4 %collective-permute-start.1 = (bf16[384,1536]{1,0:T(8,128)(2,1)S(1)}, bf16[384,1536]{1,0:T(8,128)(2,1)}, u32[]{:S(2)}, u32[]{:S(2)}) collective-permute-start(bf16[384,1536]{1,0:T(8,128)(2,1)S(1)} %get-tuple-element.131.own_in), channel_id=1, source_target_pairs={{0,64},{64,0},{1,65},{65,1},{2,66},{66,2},{3,67},{67,3},{4,68},{68... | collective-permute-start | bytes 3538952 | tf_op jit(solution)/shard_map/ppermute | solution.py:35
  5.3 40.5 %copy-start.5 = (bf16[1536,384]{1,0:T(8,128)(2,1)}, bf16[1536,384]{1,0:T(8,128)(2,1)S(1)}, u32[]{:S(2)}) copy-start(bf16[1536,384]{1,0:T(8,128)(2,1)S(1)} %get-tuple-element.129.own_out) | copy-start | bytes 3538948
  5.3 2.7 copy-start.16
  5.3 2.8 copy-start.12
  5.4 4.1 %copy-start.11 = (bf16[2,12,3,384]{3,0,2,1:T(2,128)(2,1)S(1)}, bf16[2,12,3,384]{3,0,2,1:T(2,128)(2,1)}, u32[]{:S(2)}) copy-start(bf16[2,12,3,384]{3,0,2,1:T(2,128)(2,1)} %param.14) | copy-start | bytes 165892
  5.4 4.1 %copy-start.13 = (bf16[2,384,12]{1,0,2:T(2,128)(2,1)S(1)}, bf16[2,384,12]{1,0,2:T(2,128)(2,1)}, u32[]{:S(2)}) copy-start(bf16[2,384,12]{1,0,2:T(2,128)(2,1)} %param.15) | copy-start | bytes 55300
  5.4 4.3 %copy-start.15 = (bf16[2,12,32]{2,0,1:T(2,128)(2,1)S(1)}, bf16[2,12,32]{2,0,1:T(2,128)(2,1)}, u32[]{:S(2)}) copy-start(bf16[2,12,32]{2,0,1:T(2,128)(2,1)} %param.16) | copy-start | bytes 4612
  5.4 4.3 %copy-start.18 = (bf16[2,3,12]{2,0,1:T(2,128)(2,1)S(1)}, bf16[2,3,12]{2,0,1:T(2,128)(2,1)}, u32[]{:S(2)}) copy-start(bf16[2,3,12]{2,0,1:T(2,128)(2,1)} %param.18) | copy-start | bytes 436
  5.4 4.4 %copy-start.3 = (bf16[2,2,12]{2,1,0:T(2,128)(2,1)S(1)}, bf16[2,2,12]{2,1,0:T(2,128)(2,1)}, u32[]{:S(2)}) copy-start(bf16[2,2,12]{2,1,0:T(2,128)(2,1)} %gains.1) | copy-start | bytes 292
  5.4 45.7 %collective-permute-start.2 = (bf16[1536,384]{1,0:T(8,128)(2,1)S(1)}, bf16[1536,384]{1,0:T(8,128)(2,1)}, u32[]{:S(2)}, u32[]{:S(2)}) collective-permute-start(bf16[1536,384]{1,0:T(8,128)(2,1)S(1)} %get-tuple-element.129.own_out), channel_id=1, source_target_pairs={{0,64},{64,0},{1,65},{65,1},{2,66},{66,2},{3,67},{67,3},{4,68},{68... | collective-permute-start | bytes 3538952 | tf_op jit(solution)/shard_map/ppermute | solution.py:35
  5.7 98.9 %collective-permute-start.3 = (bf16[384,1536]{1,0:T(8,128)(2,1)}, bf16[384,1536]{1,0:T(8,128)(2,1)}, u32[]{:S(2)}, u32[]{:S(2)}) collective-permute-start(bf16[384,1536]{1,0:T(8,128)(2,1)} %get-tuple-element.130.own_in), channel_id=1, source_target_pairs={{0,64},{64,0},{1,65},{65,1},{2,66},{66,2},{3,67},{67,3},{4,68},{68... | collective-permute-start | bytes 3538952 | tf_op jit(solution)/shard_map/ppermute | solution.py:35
  6.0 44.5 %copy-start.19 = (bf16[2,1,384]{2,0,1:T(2,128)(2,1)S(1)}, bf16[2,1,384]{2,0,1:T(2,128)(2,1)}, u32[]{:S(2)}) copy-start(bf16[2,1,384]{2,0,1:T(2,128)(2,1)} %param.22) | copy-start | bytes 4612
  6.0 98.5 %collective-permute-start.4 = (bf16[1536,384]{1,0:T(8,128)(2,1)}, bf16[1536,384]{1,0:T(8,128)(2,1)}, u32[]{:S(2)}, u32[]{:S(2)}) collective-permute-start(bf16[1536,384]{1,0:T(8,128)(2,1)} %get-tuple-element.128.own_out), channel_id=1, source_target_pairs={{0,64},{64,0},{1,65},{65,1},{2,66},{66,2},{3,67},{67,3},{4,68},{68... | collective-permute-start | bytes 3538952 | tf_op jit(solution)/shard_map/ppermute | solution.py:35
  45.8 1.2 copy-start
  47.0 1.7 copy-start.1
  48.8 1.7 copy-start.2
  256.8 47.1 %copy-start.7 = (f32[208,768]{1,0:T(8,128)S(1)}, f32[208,768]{1,0:T(8,128)}, u32[]{:S(2)}) copy-start(f32[208,768]{1,0:T(8,128)} %get-tuple-element.90) | copy-start | bytes 1916932
  298.9 5.8 %copy-start.10 = (f32[2,12,3,384]{3,2,1,0:T(4,128)S(1)}, f32[2,12,3,384]{3,2,1,0:T(4,128)}, u32[]{:S(2)}) copy-start(f32[2,12,3,384]{3,2,1,0:T(4,128)} %get-tuple-element.119) | copy-start | bytes 331780
  305.4 8.2 %slice-start = ((s8[4718592]{0:T(1024)(128)(4,1)}), s8[524288]{0:T(1024)(128)(4,1)S(1)}, s32[]{:S(2)}) async-start(s8[4718592]{0:T(1024)(128)(4,1)} %bitcast.32), calls=%async_computation | async-start | bytes 1048576
  308.0 5.0 %copy-start.14 = (f32[2,1,1536]{2,1,0:T(1,128)S(1)}, f32[2,1,1536]{2,1,0:T(1,128)}, u32[]{:S(2)}) copy-start(f32[2,1,1536]{2,1,0:T(1,128)} %get-tuple-element.159) | copy-start | bytes 36868
  308.0 5.6 %slice-start.1 = ((s8[4718592]{0:T(1024)(128)(4,1)}), s8[4194304]{0:T(1024)(128)(4,1)S(1)}, s32[]{:S(2)}) async-start(s8[4718592]{0:T(1024)(128)(4,1)} %bitcast.32), calls=%async_computation.1 | async-start | bytes 8388608
  313.6 2.2 copy-start.17
